TPU v7x, 512 devices: a whole 4x4x16 slice. The times are simulated.
512 devices in a mesh: pulse: 4 (over y), tile: 32 (over z, core), row: 4 (over x).
Axes of the slice: x: 4, y: 4, z: 16, core: 2. Of those that a mesh axis runs over, the one named last changes fastest.
Arguments:
- raw_pulses: float32 [2, 8192, 8192], P(None, ('pulse', 'tile', 'row')), may hold values from -6 to 6
- range_weight: float32 [8192], replicated, may hold values from 0.25 to 1.75
- visibility: int32 [32, 512], replicated, may hold values from 0 to 1, as said below
- offsets: int32 [32, 512], replicated, may hold values from 0 to 60
- doppler_rate: int32 [32], replicated, may hold values from 1 to 4095
- phase_error: float32 [32, 16], replicated, may hold values from -3.140625 to 3.140625
- row_groups: int32 [512], replicated, may hold values from 0 to 15, never falling along the last dimension, each value on 1 to 64 neighbouring positions
Outputs:
- focused: float32 [32, 512, 1024], P('tile', ('pulse', 'row'))
Inputs may be any that keep to these rules, and one draw needn't show every extreme that they name: `visibility`: write block b = (p * 32 + s) * 4 + w with p < 4, s < 32, w < 4. For every tile and every pair p, w, the tile sees at least 8 and at most 16 of the 32 blocks with that p and w; in every draw some tile sees exactly 16 of them for every p and w.
All inputs are finite; a program needn't handle non-finite values.
Results may differ from a plain program's by a relative error of at most 0.018.
Values may be sent and summed in bfloat16 or wider, within the bound.
A program may use at most 64 MiB of HBM per device.

v0:
```python
from functools import partial
import math

import jax
import jax.numpy as jnp
from jax import lax
from jax.sharding import PartitionSpec as P

R1 = 64
TILE_COLS = 512


modulus = 4096
two_pi = 2.0 * math.pi


def as_sent(shard):
    return jax.tree.map(lambda a: a.astype(jnp.bfloat16) if a.dtype == jnp.float32 else a, shard)


def dft_table(row_total, col_total, period):
    row_index = lax.broadcasted_iota(jnp.int32, (row_total, col_total), 0)
    col_index = lax.broadcasted_iota(jnp.int32, (row_total, col_total), 1)
    angles = (row_index * col_index % period).astype(jnp.float32) * (-two_pi / period)
    return (jnp.cos(angles), jnp.sin(angles))


def complex_einsum(pattern, left_pair, right_pair):
    left_re, left_im = left_pair
    right_re, right_im = right_pair
    product = partial(jnp.einsum, pattern, precision=lax.Precision.HIGHEST)
    return (
        product(left_re, right_re) - product(left_im, right_im),
        product(left_re, right_im) + product(left_im, right_re),
    )


def compress(raw_pulses, range_weight):
    pulses = raw_pulses.shape[1]
    length = raw_pulses.shape[2]
    first_factor = R1
    second_factor = length // first_factor
    signal_re = (raw_pulses[0] * range_weight).reshape(pulses, first_factor, second_factor)
    signal_im = (raw_pulses[1] * range_weight).reshape(pulses, first_factor, second_factor)
    section_re, section_im = complex_einsum(
        "kn,pnm->pkm", dft_table(first_factor, first_factor, first_factor), (signal_re, signal_im)
    )
    twist_re, twist_im = dft_table(first_factor, second_factor, length)
    section_re, section_im = (
        section_re * twist_re - section_im * twist_im,
        section_re * twist_im + section_im * twist_re,
    )
    final_re, final_im = complex_einsum(
        "jm,pkm->pjk",
        dft_table(second_factor, second_factor, second_factor),
        (section_re, section_im),
    )
    norm_value = 1.0 / math.sqrt(length)
    return (
        (final_re.reshape(pulses, length) * norm_value).astype(jnp.bfloat16),
        (final_im.reshape(pulses, length) * norm_value).astype(jnp.bfloat16),
    )


def phase_pair(row_ids, pulse_ids, rate):
    step_phase = pulse_ids * rate % modulus
    ticks = row_ids[:, None, None] * step_phase[None] % modulus
    angles = ticks.astype(jnp.float32) * (two_pi / modulus)
    cosine = jnp.cos(angles)
    sine = jnp.sin(angles)
    row_count = row_ids.shape[0]
    real_part = jnp.stack([cosine, -sine], axis=2).reshape(row_count, -1).astype(jnp.bfloat16)
    imag_part = jnp.stack([sine, cosine], axis=2).reshape(row_count, -1).astype(jnp.bfloat16)
    return (real_part, imag_part)


def focus_matrix(errors, groups, sub_rows):
    row_index = lax.broadcasted_iota(jnp.int32, (sub_rows, sub_rows), 0)
    col_index = lax.broadcasted_iota(jnp.int32, (sub_rows, sub_rows), 1)
    base_angle = (row_index * col_index % sub_rows).astype(jnp.float32) * (-two_pi / sub_rows)
    labels = jnp.arange(errors.shape[0], dtype=jnp.int32)
    row_phase = jnp.sum(jnp.where(groups[:, None] == labels[None, :], errors[None, :], 0.0), axis=1)
    angles = base_angle + row_phase[None, :]
    norm_value = 1.0 / math.sqrt(sub_rows)
    return (jnp.cos(angles) * norm_value, jnp.sin(angles) * norm_value)


def complex_rows(mat_re, mat_im, field):
    width = field.shape[1] // 2
    field_re = field[:, :width]
    field_im = field[:, width:]
    precise = partial(jnp.dot, precision=lax.Precision.HIGHEST)
    out_re = precise(mat_re, field_re) - precise(mat_im, field_im)
    out_im = precise(mat_re, field_im) + precise(mat_im, field_re)
    return jnp.concatenate([out_re, out_im], axis=1)


def body(raw_pulses, range_weight, visibility, offsets, doppler_rate, phase_error, row_groups):
    tile_count = lax.axis_size("tile")
    row_devices = lax.axis_size("row")
    group_count = lax.axis_size("pulse")
    pulses = raw_pulses.shape[1]
    tile_rows = row_groups.shape[0]
    sub_rows = tile_rows // group_count
    own_rows = sub_rows // row_devices
    range_step = TILE_COLS // 4
    pulse_group = lax.axis_index("pulse")
    tile_owner = lax.axis_index("tile")
    row_member = lax.axis_index("row")
    own_block = (pulse_group * tile_count + tile_owner) * row_devices + row_member
    comp_re, comp_im = compress(raw_pulses, range_weight)
    first_bins = offsets[:, own_block] * range_step

    def window_at(first_bin):
        return jnp.stack(
            [
                lax.dynamic_slice_in_dim(comp_re, first_bin, TILE_COLS, 1),
                lax.dynamic_slice_in_dim(comp_im, first_bin, TILE_COLS, 1),
            ]
        )

    windows = jax.vmap(window_at)(first_bins)
    windows = windows * visibility[:, own_block].astype(jnp.bfloat16)[:, None, None, None]
    received = lax.all_to_all(
        as_sent(windows), "tile", split_axis=0, concat_axis=0, tiled=True
    ).astype(windows.dtype)
    sources = (
        pulse_group * tile_count + jnp.arange(tile_count, dtype=jnp.int32)
    ) * row_devices + row_member
    rate = doppler_rate[tile_owner]
    norm_factor = 1.0 / math.sqrt(pulses * group_count * tile_count * row_devices)
    pulse_offsets = jnp.arange(pulses, dtype=jnp.int32)
    groups_here = lax.dynamic_slice_in_dim(row_groups, pulse_group * sub_rows, sub_rows)
    focus_re, focus_im = focus_matrix(phase_error[tile_owner], groups_here, sub_rows)
    row_ids = jnp.arange(lax.axis_size(("pulse", "row")) * own_rows, dtype=jnp.int32)
    stacked = received.reshape(-1, TILE_COLS)
    phase_re, phase_im = phase_pair(
        row_ids, sources[:, None] * pulses + pulse_offsets[None, :], rate
    )
    summed = jnp.concatenate(
        [
            jnp.dot(phase_re, stacked, preferred_element_type=jnp.float32),
            jnp.dot(phase_im, stacked, preferred_element_type=jnp.float32),
        ],
        axis=1,
    )
    image_share = lax.psum_scatter(
        (summed * norm_factor).astype(jnp.bfloat16),
        ("pulse", "row"),
        scatter_dimension=0,
        tiled=True,
    )
    own_re = lax.dynamic_slice_in_dim(focus_re, row_member * own_rows, own_rows, 0)
    own_im = lax.dynamic_slice_in_dim(focus_im, row_member * own_rows, own_rows, 0)
    start_value = jnp.zeros((own_rows, 2 * TILE_COLS), jnp.float32)
    focused = start_value + complex_rows(
        own_re, own_im, lax.all_gather(image_share, "row", axis=0, tiled=True).astype(jnp.float32)
    )
    return focused[None]


def solution(mesh):
    return jax.shard_map(
        body,
        mesh=mesh,
        in_specs=(P(None, ("pulse", "tile", "row"), None), P(), P(), P(), P(), P(), P()),
        out_specs=P("tile", ("pulse", "row"), None),
        check_vma=False,
    )
```

profile of v0, /device:TPU:1, one launch (start us, length us, event | category | flops | bytes accessed | tf_op | source)
XLA Modules:
  0.0 275.6 jit_solution(10617676028346706544)
XLA Ops:
  6.7 1.3 slice_bitcast_fusion.1
  8.9 0.7 fusion.54
  9.6 0.7 fusion.52
  10.4 0.7 fusion.4
  11.1 0.7 fusion.3
  11.9 0.8 fusion.26
  12.7 0.8 fusion.27
  13.5 0.8 fusion.8
  15.4 42.0 %while.2 = (s32[]{:T(128)}, bf16[16,8192]{1,0:T(8,128)(2,1)S(1)}, s32[32,2]{0,1:T(2,128)S(1)}, bf16[32,16,512]{2,1,0:T(8,128)(2,1)S(1)}, s32[]{:T(128)}) while((s32[]{:T(128)}, bf16[16,8192]{1,0:T(8,128)(2,1)S(1)}, s32[32,2]{0,1:T(2,128)S(1)}, bf16[32,16,512]{2,1,0:T(8,128)(2,1)S(1)}, s32[]{:T(128)}) %tuple.35), condition=%wide.while_cond, body=%wide.while_body.sunk | while | flops 2 | bytes 32865 | solution.py:117
  16.0 0.7 bitcast_dynamic-update-slice_fusion.4
  18.6 0.7 bitcast_dynamic-update-slice_fusion.4
  21.2 0.7 bitcast_dynamic-update-slice_fusion.4
  22.6 0.7 bitcast_dynamic-update-slice_fusion.4
  25.2 0.7 bitcast_dynamic-update-slice_fusion.4
  26.5 0.7 bitcast_dynamic-update-slice_fusion.4
  29.1 0.7 bitcast_dynamic-update-slice_fusion.4
  31.7 0.7 bitcast_dynamic-update-slice_fusion.4
  33.0 0.7 bitcast_dynamic-update-slice_fusion.4
  35.7 0.7 bitcast_dynamic-update-slice_fusion.4
  57.3 0.8 fusion.7
  59.0 42.0 %while.3 = (s32[]{:T(128)}, bf16[16,8192]{1,0:T(8,128)(2,1)S(1)}, s32[32,2]{0,1:T(2,128)S(1)}, bf16[32,16,512]{2,1,0:T(8,128)(2,1)S(1)}, s32[]{:T(128)}) while((s32[]{:T(128)}, bf16[16,8192]{1,0:T(8,128)(2,1)S(1)}, s32[32,2]{0,1:T(2,128)S(1)}, bf16[32,16,512]{2,1,0:T(8,128)(2,1)S(1)}, s32[]{:T(128)}) %tuple.40), condition=%wide.while_cond.1, body=%wide.while_body.1.sunk | while | flops 2 | bytes 32865 | solution.py:118
  101.0 0.9 fusion.77
  101.9 1.1 fusion.15
  103.0 16.9 %all-to-all-start = ((bf16[32,2,16,512]{3,2,1,0:T(8,128)(2,1)}), bf16[32,2,16,512]{3,2,1,0:T(8,128)(2,1)S(1)}, u32[]{:S(2)}, u32[]{:S(2)}) async-start(bf16[32,2,16,512]{3,2,1,0:T(8,128)(2,1)} %fusion.15), calls=%async_computation | async-start | bytes 2097152 | tf_op jit(solution)/shard_map/all_to_all | solution.py:124
  121.2 4.9 %negate_convert_fusion = (bf16[512,32,1,16]{0,1,3,2:T(8,128)(2,1)S(1)}, bf16[512,32,1,16]{0,1,3,2:T(8,128)(2,1)S(1)}, bf16[512,32,1,16]{0,1,3,2:T(8,128)(2,1)S(1)}) fusion(s32[32,16]{0,1:T(8,128)S(1)} %add_select_fusion.4), kind=kLoop, calls=%fused_computation.36 | loop fusion | flops 4718592 | bytes 1574912 | tf_op jit(solution)/shard_map/convert.3
  126.1 49.5 %all-to-all-done = bf16[32,2,16,512]{3,2,1,0:T(8,128)(2,1)S(1)} async-done(((bf16[32,2,16,512]{3,2,1,0:T(8,128)(2,1)}), bf16[32,2,16,512]{3,2,1,0:T(8,128)(2,1)S(1)}, u32[]{:S(2)}, u32[]{:S(2)}) %all-to-all-start) | async-done | bytes 1048608 | tf_op jit(solution)/shard_map/all_to_all | solution.py:124
  175.6 0.9 convolution_bitcast_fusion.1
  176.5 0.9 convolution_bitcast_fusion
  177.8 1.3 copy.30
  179.1 0.8 dynamic_slice.21
  180.2 77.4 %reduce-scatter.4.cloned.1.call-done = bf16[32,1024]{1,0:T(8,128)(2,1)} async-done(((bf16[512,1024]{1,0:T(8,128)(2,1)}), bf16[32,1024]{1,0:T(8,128)(2,1)}) %reduce-scatter.4.cloned.1.call-update) | async-done | bytes 65552 | tf_op jit(solution)/shard_map/reduce_scatter | solution.py:147
  257.5 9.6 %all_gather.3 = bf16[128,1024]{1,0:T(8,128)(2,1)S(1)} all-gather(bf16[32,1024]{1,0:T(8,128)(2,1)} %reduce-scatter.4.cloned.1.call-done), channel_id=1, replica_groups=mesh['pulse'=4,'tile'=32,'row'=4] {'row'}, dimensions={0}, use_global_device_ids=true | all-gather | bytes 327680 | tf_op jit(solution)/shard_map/all_gather | solution.py:157
  (218 shorter events, 83.2 us)
Async XLA Ops:
  6.5 8.6 %copy-start = (s32[32,512]{1,0:T(8,128)S(1)}, s32[32,512]{1,0:T(8,128)}, u32[]{:S(2)}) copy-start(s32[32,512]{1,0:T(8,128)} %param.10) | copy-start | bytes 196612
  8.0 0.8 copy-start.1
  103.0 16.9 %copy-start.3 = (s32[32]{0:T(128)S(1)}, s32[32]{0:T(128)}, u32[]{:S(2)}) copy-start(s32[32]{0:T(128)} %param.11) | copy-start | bytes 388
  103.0 72.6 %all-to-all-start = ((bf16[32,2,16,512]{3,2,1,0:T(8,128)(2,1)}), bf16[32,2,16,512]{3,2,1,0:T(8,128)(2,1)S(1)}, u32[]{:S(2)}, u32[]{:S(2)}) async-start(bf16[32,2,16,512]{3,2,1,0:T(8,128)(2,1)} %fusion.15), calls=%async_computation | async-start | bytes 2097152 | tf_op jit(solution)/shard_map/all_to_all | solution.py:124
  119.9 137.7 %reduce-scatter.4.cloned.1.call-start = ((), (), s32[]{:S(2)}) async-start(), calls=%async_computation.2 | async-start | bytes 1114112 | tf_op jit(solution)/shard_map/reduce_scatter | solution.py:147
  179.1 0.8 copy-start.2
Sparse Core Ops, SparseCore 0:
  179.2 78.2 reduce-scatter.3
where the time goes:
time: 280 us; the launch traced here: 276 us
  waiting for transfers between devices  127 us (45%)
  local copies, waits for them, and re-layouts  90.4 us (32%)
  starting transfers between devices  16.9 us (6%)
  between operations  13.6 us (5%)
  blocking collectives  9.57 us (3%)
  matrix products  9.05 us (3%)
  other arithmetic  9.01 us (3%)
    gather x192, local copies, waits for them, and re-layouts  83.8 us
    reduce_scatter x1, waiting for transfers between devices, body(): lax.psum_scatter((summed * norm_factor).astype(jnp.bfloat16), ('pulse', '...  77.4 us
    all_to_all x1, waiting for transfers between devices, body(): lax.all_to_all(as_sent(windows), 'tile', split_axis=0, concat_axis=0, til...  49.5 us
    all_to_all x1, starting transfers between devices, body(): lax.all_to_all(as_sent(windows), 'tile', split_axis=0, concat_axis=0, til...  16.9 us
    all_gather x1, blocking collectives, body(): lax.all_gather(image_share, 'row', axis=0, tiled=True).astype(jnp.float32)  9.57 us
  transfers between devices with their start and end apart: 2, of which 2 were waited for; matrix products, arithmetic and copies ran while one was open for 3% of the time, Pallas kernels for 0%

commit v1 on v0

v1 whole, which is shorter than its diff:
```python
from functools import partial
import math

import numpy as np
import jax
import jax.numpy as jnp
from jax import lax
from jax.experimental import pallas as pl
from jax.experimental.pallas import tpu as pltpu
from jax.sharding import PartitionSpec as P

MESH = pl.DeviceIdType.MESH
F32 = jnp.float32
BF16 = jnp.bfloat16
NSUB = 2

TWO_PI = 2.0 * math.pi


def dft_tables():
    n1, v = np.arange(128)[:, None], np.arange(128)[None, :]
    a = TWO_PI * (n1 * v % 128) / 128
    c, s = np.cos(a), np.sin(a)
    first = np.block([[c, -s], [s, c]]).astype(np.float32)
    n2 = np.arange(64)[:, None]
    t = TWO_PI * (n2 * v % 8192) / 8192
    twist = np.stack([np.cos(t), -np.sin(t)]).astype(np.float32)
    u = np.arange(64)[:, None]
    b = TWO_PI * (u * np.arange(64)[None, :] % 64) / 64
    second = np.concatenate([np.cos(b), np.sin(b)], axis=1).astype(np.float32)
    focus = np.block([[c, s], [-s, c]]).astype(np.float32)
    return first, twist, second, focus


def swap_bits(blocks, low):
    blocks = list(blocks)
    lane = lax.broadcasted_iota(jnp.int32, blocks[0].shape, 1)
    bit = 1
    while bit < len(blocks):
        shift = bit << low
        high = (lane & shift) != 0
        for i in range(len(blocks)):
            if i & bit == 0:
                a, b = blocks[i], blocks[i | bit]
                blocks[i] = jnp.where(high, pltpu.roll(b, shift, 1), a)
                blocks[i | bit] = jnp.where(high, b, pltpu.roll(a, 128 - shift, 1))
        bit *= 2
    return blocks


def unit_root(ticks, period):
    x = ticks.astype(F32) * (1.0 / period)
    x = x - jnp.where(x >= 0.5, 1.0, 0.0)
    h = x * math.pi
    q = h * h
    sh = h * (1.0 + q * (-1 / 6 + q * (1 / 120 + q * (-1 / 5040 + q * (1 / 362880)))))
    ch = 1.0 + q * (-1 / 2 + q * (1 / 24 + q * (-1 / 720 + q * (1 / 40320 + q * (-1 / 3628800)))))
    return 1.0 - 2.0 * sh * sh, 2.0 * sh * ch


def compress_kernel(x_ref, first_ref, twist_ref, second_ref, out_ref, mid, spec):
    hp = lax.Precision.HIGHEST
    x = jnp.concatenate([x_ref[0], x_ref[1]], axis=1)
    mid[...] = jnp.dot(x, first_ref[...], precision=hp, preferred_element_type=F32)
    t_re, t_im = twist_ref[0], twist_ref[1]
    norm = 1.0 / math.sqrt(8192)

    def pulse(j, carry):
        y = mid[pl.ds(pl.multiple_of(j * 64, 64), 64), :]
        y_re, y_im = y[:, :128], y[:, 128:]
        b_re = y_re * t_re - y_im * t_im
        b_im = y_re * t_im + y_im * t_re
        right = jnp.concatenate(
            [jnp.concatenate([b_re, b_im], axis=1), jnp.concatenate([b_im, -b_re], axis=1)], axis=0
        )
        z = jnp.dot(second_ref[...], right, precision=hp, preferred_element_type=F32) * norm
        spec[j] = z[:, :128]
        spec[j + 16] = z[:, 128:]
        return carry

    lax.fori_loop(0, 16, pulse, 0)

    def rows(g, carry):
        at = pl.ds(pl.multiple_of(g * 8, 8), 8)
        blocks = swap_bits([spec[i, at, :] for i in range(32)], 0)
        for i in range(32):
            spec[i, at, :] = blocks[i]
        return carry

    lax.fori_loop(0, 8, rows, 0)

    def cast(i, carry):
        out_ref[i] = spec[i].astype(BF16)
        return carry

    lax.fori_loop(0, 32, cast, 0)


def compress(signal, first, twist, second):
    return pl.pallas_call(
        compress_kernel,
        out_shape=jax.ShapeDtypeStruct((32, 64, 128), BF16),
        in_specs=[pl.BlockSpec(memory_space=pltpu.VMEM)] * 4,
        out_specs=pl.BlockSpec(memory_space=pltpu.VMEM),
        scratch_shapes=[pltpu.VMEM((1024, 256), F32), pltpu.VMEM((32, 64, 128), F32)],
        compiler_params=pltpu.CompilerParams(vmem_limit_bytes=40 * 2**20),
    )(signal, first, twist, second)


def image_kernel(
    rate_ref, msg_ref, spots_ref, error_ref, focus_ref, out_ref,
    recv, pick, gath, weight, phase, part_a, part_b, send_a, send_b, recv_a, recv_b, msg2, recv2,
    sem_s1, sem_r1, sem_sa, sem_ra, sem_sb, sem_rb, sem_s2, sem_r2,
):
    py = lax.axis_index("pulse")
    zc = lax.axis_index("tile")
    wx = lax.axis_index("row")
    z, core = zc // 2, zc % 2
    me = py * 8 + wx * 2 + core

    def slot_of(p, w, c):
        return (((p % 2) * 4 + w) * 2 + c) * 2 + p // 2

    own_slot = slot_of(py, wx, core)
    up = (py, ((z + 1) % 16) * 2 + core, wx)
    down = (py, ((z + 15) % 16) * 2 + core, wx)

    def to_peer(d):
        return (py + d // 8) % 4, (wx + (d // 2) % 4) % 4, (core + d % 2) % 2

    def from_peer(d):
        return (py + 4 - d // 8) % 4, (wx + 4 - (d // 2) % 4) % 4, (core + d % 2) % 2

    barrier = pltpu.get_barrier_semaphore()

    def greet(d, carry):
        p, w, c = to_peer(d)
        pl.semaphore_signal(barrier, inc=1, device_id=(p, z * 2 + c, w), device_id_type=MESH)
        return carry

    lax.fori_loop(1, 32, greet, 0)
    pl.semaphore_signal(barrier, inc=1, device_id=up, device_id_type=MESH)
    pl.semaphore_signal(barrier, inc=1, device_id=down, device_id_type=MESH)
    pl.semaphore_wait(barrier, 33)

    def first_copy(d):
        p, w, c = to_peer(d)
        return pltpu.make_async_remote_copy(
            src_ref=msg_ref.at[p * 8 + w * 2 + c],
            dst_ref=recv.at[own_slot],
            send_sem=sem_s1.at[d],
            recv_sem=sem_r1.at[own_slot],
            device_id=(p, z * 2 + c, w),
            device_id_type=MESH,
        )

    def first_arrival(d):
        p, w, c = from_peer(d)
        slot = slot_of(p, w, c)
        return pltpu.make_async_remote_copy(
            src_ref=msg_ref.at[0],
            dst_ref=recv.at[slot],
            send_sem=sem_s1.at[d],
            recv_sem=sem_r1.at[slot],
            device_id=(p, z * 2 + c, w),
            device_id_type=MESH,
        )

    def start_first(d, carry):
        first_copy(d).start()
        return carry

    lax.fori_loop(1, 32, start_first, 0)
    recv[own_slot] = msg_ref[me]

    def spots(i, carry):
        key = lax.broadcasted_iota(jnp.int32, (128, 256), 0)
        lane = lax.broadcasted_iota(jnp.int32, (128, 256), 1)
        chosen = jnp.where(key == i * 4 + lane // 64, 1.0, 0.0).astype(BF16)
        place = jnp.dot(spots_ref[...], chosen, preferred_element_type=F32)
        unit = (lax.broadcasted_iota(jnp.int32, (256, 256), 1) % 64).astype(F32)
        pick[i] = jnp.where(place == unit, 1.0, 0.0).astype(BF16)
        return carry

    lax.fori_loop(0, 8, spots, 0)

    def azimuth(t, carry):
        rate = rate_ref[t]
        low = lax.broadcasted_iota(jnp.int32, (8, 512), 0)
        row = lax.broadcasted_iota(jnp.int32, (8, 512), 1)
        step = (low * rate) & 4095
        a_re, a_im = unit_root((step * row) & 4095, 4096)
        b_re, b_im = unit_root((((step * 8) & 4095) * row) & 4095, 4096)
        for w in range(4):
            parts_re, parts_im = [], []
            for k in (2 * w, 2 * w + 1):
                k_re, k_im = b_re[k:k + 1, :], b_im[k:k + 1, :]
                parts_re.append(a_re * k_re - a_im * k_im)
                parts_im.append(a_re * k_im + a_im * k_re)
            e_re = jnp.concatenate(parts_re, axis=0)
            e_im = jnp.concatenate(parts_im, axis=0)
            weight[t, w * 32:w * 32 + 16, 0:512] = e_re.astype(BF16)
            weight[t, w * 32:w * 32 + 16, 512:1024] = e_im.astype(BF16)
            weight[t, w * 32 + 16:w * 32 + 32, 0:512] = (-e_im).astype(BF16)
            weight[t, w * 32 + 16:w * 32 + 32, 512:1024] = e_re.astype(BF16)
        sub = lax.broadcasted_iota(jnp.int32, (8, 128), 0)
        lane = lax.broadcasted_iota(jnp.int32, (8, 128), 1)
        for p2 in range(2):
            sigma = p2 * 32 + z * 2 + sub // 4
            s_re, s_im = unit_root((((sigma * rate) & 63) * lane) & 63, 64)
            phase[t, 2 * p2] = s_re
            phase[t, 2 * p2 + 1] = s_im
        return carry

    lax.fori_loop(0, 32, azimuth, 0)

    def await_first(d, carry):
        first_arrival(d).wait_recv()
        return carry

    lax.fori_loop(1, 32, await_first, 0)

    def gather(p2, carry):
        found = []
        for w in range(4):
            slot = pl.multiple_of((p2 * 4 + w) * 4, 4)
            data = recv[pl.ds(slot, 4)].reshape(256, 128)
            found.append(jnp.dot(pick[p2 * 4 + w], data, preferred_element_type=F32))
        for t in range(32):
            rows = slice(t * 8, t * 8 + 8)
            blocks = swap_bits([f[rows, :] for f in found], 5)
            for vi in range(4):
                gath[t, vi * 2 + p2] = blocks[vi]
        return carry

    lax.fori_loop(0, 2, gather, 0)

    def partial_image(dest, store):
        sub = lax.broadcasted_iota(jnp.int32, (8, 128), 0) < 4
        sums = []
        for k in range(2):
            t = dest * 2 + k
            left = gath[t].reshape(64, 128).astype(BF16)
            y = jnp.dot(left, weight[t], preferred_element_type=F32)
            s = [phase[t, i] for i in range(4)]
            mine = {}
            for g in range(4):
                for vi in range(4):
                    tot_re = tot_im = None
                    for p2 in range(2):
                        rows = slice((vi * 2 + p2) * 8, (vi * 2 + p2) * 8 + 8)
                        y_re = y[rows, g * 128:g * 128 + 128]
                        y_im = y[rows, 512 + g * 128:640 + g * 128]
                        r = y_re * s[2 * p2] - y_im * s[2 * p2 + 1]
                        i = y_re * s[2 * p2 + 1] + y_im * s[2 * p2]
                        tot_re = r if tot_re is None else tot_re + r
                        tot_im = i if tot_im is None else tot_im + i
                    mine[0, g, vi] = tot_re + pltpu.roll(tot_re, 4, 0)
                    mine[1, g, vi] = tot_im + pltpu.roll(tot_im, 4, 0)
            sums.append(mine)
        for ri in range(2):
            for g in range(4):
                for vi in range(4):
                    both = jnp.where(sub, sums[0][ri, g, vi], sums[1][ri, g, vi])
                    at = ri * 512 + g * 128
                    store[vi * 8:vi * 8 + 8, at:at + 128] = both

    rows_sub = 32 // NSUB

    def ring_copy(src, dst, send_sem, recv_sem, step, h, peer):
        rows = pl.ds(h * rows_sub, rows_sub)
        return pltpu.make_async_remote_copy(
            src_ref=src.at[step, rows, :],
            dst_ref=dst.at[step, rows, :],
            send_sem=send_sem.at[step, h],
            recv_sem=recv_sem.at[step, h],
            device_id=peer,
            device_id_type=MESH,
        )

    def copy_a(step, h):
        return ring_copy(send_a, recv_a, sem_sa, sem_ra, step, h, up)

    def copy_b(step, h):
        return ring_copy(send_b, recv_b, sem_sb, sem_rb, step, h, down)

    def ring_step(s, carry):
        partial_image((z + 8 - s) % 16, part_a)
        partial_image((z + 9 + s) % 16, part_b)

        @pl.when(s == 0)
        def _():
            send_a[0] = part_a[...].astype(BF16)
            send_b[0] = part_b[...].astype(BF16)
            for h in range(NSUB):
                copy_a(0, h).start()
                copy_b(0, h).start()

        @pl.when(s > 0)
        def _():
            for h in range(NSUB):
                rows = slice(h * rows_sub, (h + 1) * rows_sub)
                copy_a(s - 1, h).wait_recv()
                send_a[s, rows, :] = (part_a[rows, :] + recv_a[s - 1, rows, :].astype(F32)).astype(BF16)
                copy_a(s, h).start()

                copy_b(s - 1, h).wait_recv()
                send_b[s, rows, :] = (part_b[rows, :] + recv_b[s - 1, rows, :].astype(F32)).astype(BF16)

                @pl.when(s < 7)
                def _():
                    copy_b(s, h).start()
        return carry

    lax.fori_loop(0, 8, ring_step, 0)
    for h in range(NSUB):
        rows = slice(h * rows_sub, (h + 1) * rows_sub)
        copy_a(7, h).wait_recv()
        part_b[rows, :] = part_b[rows, :] + recv_b[6, rows, :].astype(F32) + recv_a[7, rows, :].astype(F32)

    rights = []
    for vi in range(4):
        for q in range(4):
            at = q * 128
            i_re = part_b[vi * 8:vi * 8 + 8, at:at + 128]
            i_im = part_b[vi * 8:vi * 8 + 8, 512 + at:640 + at]
            c, s = error_ref[0, :, at:at + 128], error_ref[1, :, at:at + 128]
            rights.append(jnp.concatenate([i_re * c - i_im * s, i_re * s + i_im * c], axis=1))
    right = (jnp.concatenate(rights, axis=0) * (1.0 / 1024)).astype(BF16)
    spun = lax.dot_general(
        focus_ref[...], right, (((1,), (1,)), ((), ())), preferred_element_type=F32
    )
    for w in range(4):
        blocks = []
        for i in range(8):
            at = (i // 4) * 128 + w * 32 + (i % 4) * 8
            blocks.append(spun[at:at + 8, :])
        blocks = swap_bits(blocks, 2)
        for i in range(8):
            msg2[(i // 2) * 8 + w * 2 + i % 2] = blocks[i]

    def last_copy(d):
        p, w, c = to_peer(d)
        return pltpu.make_async_remote_copy(
            src_ref=msg2.at[p * 8 + w * 2 + c],
            dst_ref=recv2.at[me],
            send_sem=sem_s2.at[d],
            recv_sem=sem_r2.at[me],
            device_id=(p, z * 2 + c, w),
            device_id_type=MESH,
        )

    def last_arrival(d):
        p, w, c = from_peer(d)
        k = p * 8 + w * 2 + c
        return pltpu.make_async_remote_copy(
            src_ref=msg2.at[0],
            dst_ref=recv2.at[k],
            send_sem=sem_s2.at[d],
            recv_sem=sem_r2.at[k],
            device_id=(p, z * 2 + c, w),
            device_id_type=MESH,
        )

    def start_last(d, carry):
        last_copy(d).start()
        return carry

    lax.fori_loop(1, 32, start_last, 0)
    recv2[me] = msg2[me]

    def finish_sends(d, carry):
        first_copy(d).wait_send()
        return carry

    lax.fori_loop(1, 32, finish_sends, 0)
    for s in range(8):
        for h in range(NSUB):
            copy_a(s, h).wait_send()
            if s < 7:
                copy_b(s, h).wait_send()

    def await_last(d, carry):
        last_arrival(d).wait_recv()
        return carry

    lax.fori_loop(1, 32, await_last, 0)
    blocks = swap_bits([recv2[k] for k in range(32)], 0)
    for i in range(32):
        ri, hi, unit = i // 16, (i // 4) % 4, i % 4
        at = ri * 512 + unit * 128
        out_ref[hi * 8:hi * 8 + 8, at:at + 128] = blocks[i]

    def finish_last(d, carry):
        last_copy(d).wait_send()
        return carry

    lax.fori_loop(1, 32, finish_last, 0)


def make_image(rates, messages, spots, errors, focus):
    vmem = pl.BlockSpec(memory_space=pltpu.VMEM)
    dma = pltpu.SemaphoreType.DMA
    return pl.pallas_call(
        image_kernel,
        out_shape=jax.ShapeDtypeStruct((32, 1024), F32),
        in_specs=[pl.BlockSpec(memory_space=pltpu.SMEM)] + [vmem] * 4,
        out_specs=vmem,
        scratch_shapes=[
            pltpu.VMEM((32, 64, 128), BF16),
            pltpu.VMEM((8, 256, 256), BF16),
            pltpu.VMEM((32, 8, 8, 128), F32),
            pltpu.VMEM((32, 128, 1024), BF16),
            pltpu.VMEM((32, 4, 8, 128), F32),
            pltpu.VMEM((32, 1024), F32),
            pltpu.VMEM((32, 1024), F32),
            pltpu.VMEM((8, 32, 1024), BF16),
            pltpu.VMEM((8, 32, 1024), BF16),
            pltpu.VMEM((8, 32, 1024), BF16),
            pltpu.VMEM((7, 32, 1024), BF16),
            pltpu.VMEM((32, 8, 128), F32),
            pltpu.VMEM((32, 8, 128), F32),
            dma((32,)), dma((32,)),
            dma((8, NSUB)), dma((8, NSUB)), dma((7, NSUB)), dma((7, NSUB)),
            dma((32,)), dma((32,)),
        ],
        compiler_params=pltpu.CompilerParams(
            collective_id=0, has_side_effects=True, vmem_limit_bytes=48 * 2**20
        ),
    )(rates, messages, spots, errors, focus)


def body(raw_pulses, range_weight, visibility, offsets, doppler_rate, phase_error, row_groups):
    first, twist, second, focus = dft_tables()
    z = lax.axis_index("tile") // 2
    signal = (raw_pulses * range_weight).reshape(2, 16, 128, 64).swapaxes(2, 3).reshape(2, 1024, 128)
    messages = compress(signal, jnp.asarray(first), jnp.asarray(twist), jnp.asarray(second))

    def plane(a):
        return lax.dynamic_slice_in_dim(a.reshape(32, 2, 2, 32, 4), z * 2, 2, 3)

    place = jnp.where(plane(visibility) != 0, plane(offsets), -8)
    place = place.transpose(0, 2, 4, 3, 1)
    same = jnp.eye(2, dtype=jnp.int32)[None, :, None, None, None, :, None]
    unit = jnp.arange(4, dtype=jnp.int32)[None, None, :, None, None, None, None]
    spots = jnp.where(same == 1, place[:, None, None] + unit, -8)
    spots = jnp.pad(spots.reshape(256, 32), ((0, 0), (0, 96))).astype(BF16)

    errors = lax.dynamic_slice_in_dim(phase_error, z * 2, 2, 0)
    labels = jnp.arange(16, dtype=jnp.int32)
    turn = jnp.sum(jnp.where(row_groups[None, :, None] == labels, errors[:, None, :], 0.0), axis=2)
    turn = jnp.repeat(turn, 4, axis=0)
    errors = jnp.stack([jnp.cos(turn), jnp.sin(turn)])
    focused = make_image(doppler_rate, messages, spots, errors, jnp.asarray(focus).astype(BF16))
    return focused[None]


def solution(mesh):
    return jax.shard_map(
        body,
        mesh=mesh,
        in_specs=(P(None, ("pulse", "tile", "row"), None), P(), P(), P(), P(), P(), P()),
        out_specs=P("tile", ("pulse", "row"), None),
        check_vma=False,
    )
```

time: 280 us -> 79.6 us (0.28); the launches traced: 276 us -> 79.4 us
  waiting for transfers between devices: 127 us -> 0 us
  local copies, waits for them, and re-layouts: 90.4 us -> 6.59 us
  Pallas kernels: 0 us -> 70.3 us
  starting transfers between devices: 16.9 us -> 0 us
  between operations: 13.6 us -> 0.26 us
  blocking collectives: 9.57 us -> 0 us
  matrix products: 9.05 us -> 0 us
  other arithmetic: 9.01 us -> 2.25 us
    gather x192 -> x0, local copies, waits for them, and re-layouts: 83.8 us -> none
    reduce_scatter x1 -> x0, waiting for transfers between devices: 77.4 us -> none  [body(): lax.psum_scatter((summed * norm_factor).astype(jnp.bfloat16), ('pulse', '...]
    pallas_call x0 -> x2, Pallas kernels: none -> 70.3 us  [the longest x1 62.4 us: make_image(): pl.pallas_call(image_kernel, out_shape=jax.ShapeDtypeStruct((32, 1024), F...]
    all_to_all x1 -> x0, waiting for transfers between devices: 49.5 us -> none  [body(): lax.all_to_all(as_sent(windows), 'tile', split_axis=0, concat_axis=0, til...]
    all_to_all x1 -> x0, starting transfers between devices: 16.9 us -> none  [body(): lax.all_to_all(as_sent(windows), 'tile', split_axis=0, concat_axis=0, til...]
    all_gather x1 -> x0, blocking collectives: 9.57 us -> none  [body(): lax.all_gather(image_share, 'row', axis=0, tiled=True).astype(jnp.float32)]
    dot_general x14 -> x0, matrix products: 9.05 us -> none  [the longest x2 1.58 us: complex_einsum(): product(left_im, right_im)]
    another operation x1 -> x2, other arithmetic: 4.93 us -> 0.61 us
  transfers between devices with their start and end apart: 2 -> 0, of which waited for: 2 -> 0; matrix products, arithmetic and copies ran while one was open for 3% -> 0% of each run, Pallas kernels for 0% -> 0%
where the time goes in v1:
time: 79.6 us; the launch traced here: 79.4 us
  Pallas kernels  70.3 us (88%)
  local copies, waits for them, and re-layouts  6.59 us (8%)
  other arithmetic  2.25 us (3%)
    pallas_call x1, Pallas kernels, make_image(): pl.pallas_call(image_kernel, out_shape=jax.ShapeDtypeStruct((32, 1024), F...  62.4 us
    pallas_call x1, Pallas kernels, compress(): pl.pallas_call(compress_kernel, out_shape=jax.ShapeDtypeStruct((32, 64, 1...  7.88 us
    transpose x1, local copies, waits for them, and re-layouts, body(): (raw_pulses * range_weight).reshape(2, 16, 128, 64).swapaxes(2, 3)  2.22 us
    reshape x1, local copies, waits for them, and re-layouts, body(): (raw_pulses * range_weight).reshape(2, 16, 128, 64).swapaxes(2, 3)  2.19 us

profile of v1, /device:TPU:1, one launch (start us, length us, event | category | flops | bytes accessed | tf_op | source)
XLA Modules:
  0.0 79.4 jit_solution(5137647742482327442)
XLA Ops:
  0.0 0.0 copy-start
  0.0 1.3 %broadcast_multiply_fusion = f32[2,16,8192]{2,1,0:T(8,128)S(1)} fusion(f32[2,16,8192]{2,1,0:T(8,128)} %param.11, f32[8192]{0:T(1024)} %param.12), kind=kLoop, calls=%fused_computation.2 | loop fusion | flops 262144 | bytes 2129920 | tf_op jit(solution)/shard_map/mul | solution.py:436
  1.3 2.2 %reshape.84 = f32[2,16,128,64]{3,2,1,0:T(8,128)} reshape(f32[2,16,8192]{2,1,0:T(8,128)S(1)} %broadcast_multiply_fusion) | data formatting | bytes 2097152 | tf_op jit(solution)/shard_map/reshape | solution.py:436
  3.5 0.0 copy-start.1
  3.5 0.0 copy-start.3
  3.5 0.0 copy-start.7
  3.5 2.2 %copy.21 = f32[2,16,64,128]{3,2,1,0:T(8,128)S(1)} copy(f32[2,16,64,128]{2,3,1,0:T(8,128)} %bitcast.11) | data formatting | bytes 2097152 | tf_op jit(solution)/shard_map/transpose | solution.py:436
  5.8 0.0 copy-done.1
  5.8 0.0 copy-done.3
  5.8 0.0 copy-done.4
  5.8 0.0 copy-start.8
  5.8 7.9 %shard_map.109.msg_ref = bf16[32,64,128]{2,1,0:T(8,128)(2,1)S(1)} custom-call(f32[2,1024,128]{2,1,0:T(8,128)S(1)} %bitcast.9, f32[256,256]{1,0:T(8,128)S(1)} %copy-done.1, f32[2,64,128]{2,1,0:T(8,128)S(1)} %copy-done.3, f32[64,128]{1,0:T(8,128)S(1)} %copy-done.4), custom_call_target="tpu_custom_call" | custom-call | tf_op jit(solution)/shard_map/pallas_call | solution.py:100
  13.7 0.0 copy-start.2
  13.7 0.0 copy-start.5
  13.7 0.0 copy-done.6
  13.7 0.1 copy.23
  13.9 0.0 copy-done.7
  13.9 0.1 copy.22
  14.1 0.2 iota_add_fusion
  14.3 0.6 select_convert_fusion
  14.9 0.8 %select_n.30 = bf16[256,32]{0,1:T(8,128)(2,1)S(1)} reshape(bf16[32,2,4,2,4,2,2]{2,1,0,6,5,4,3:T(2,128)(2,1)S(1)} %select_convert_fusion) | data formatting | bytes 32768 | tf_op jit(solution)/shard_map/jit(_where)/select_n | solution.py:446
  15.7 0.1 copy.25
  15.9 0.0 copy-done
  15.9 0.1 constant_dynamic-slice_fusion
  16.0 0.1 copy.26
  16.0 0.0 copy-done.8
  16.1 0.1 select_reduce_fusion
  16.1 0.1 fusion.1
  16.3 0.0 copy-done.2
  16.3 0.0 copy-done.5
  16.3 62.4 %shard_map.110 = f32[32,1024]{1,0:T(8,128)S(1)} custom-call(s32[32]{0:T(128)S(1)} %copy-done.5, bf16[32,64,128]{2,1,0:T(8,128)(2,1)S(1)} %shard_map.109.msg_ref, bf16[256,128]{1,0:T(8,128)(2,1)S(1)} %pad.5.spots_ref, f32[2,8,512]{2,1,0:T(8,128)S(1)} %pad_maximum_fusion.error_ref, bf16[256,256]{1,0:T(8,128)(2,1)S(1)} %copy-done.2), custom_call_target="tpu_custom_call" | custom-call | tf_op jit(solution)/shard_map/pallas_call | solution.py:404
  78.8 0.7 copy.28
  (12 shorter events, 0.1 us)
Async XLA Ops:
  0.0 15.9 %copy-start = (f32[32,16]{0,1:T(8,128)S(1)}, f32[32,16]{0,1:T(8,128)}, u32[]{:S(2)}) copy-start(f32[32,16]{0,1:T(8,128)} %param.16) | copy-start | bytes 6148
  3.5 2.3 %copy-start.1 = (f32[256,256]{1,0:T(8,128)S(1)}, f32[256,256]{1,0:T(8,128)}, u32[]{:S(2)}) copy-start(f32[256,256]{1,0:T(8,128)} %constant.40.clone.first_ref) | copy-start | bytes 786436
  3.5 2.3 %copy-start.3 = (f32[2,64,128]{2,1,0:T(8,128)S(1)}, f32[2,64,128]{2,1,0:T(8,128)}, u32[]{:S(2)}) copy-start(f32[2,64,128]{2,1,0:T(8,128)} %constant.41.clone.twist_ref) | copy-start | bytes 196612
  3.5 2.3 %copy-start.4 = (f32[64,128]{1,0:T(8,128)S(1)}, f32[64,128]{1,0:T(8,128)}, u32[]{:S(2)}) copy-start(f32[64,128]{1,0:T(8,128)} %constant.42.clone.second_ref) | copy-start | bytes 98308
  3.5 10.2 %copy-start.6 = (s32[32,512]{1,0:T(8,128)S(1)}, s32[32,512]{1,0:T(8,128)}, u32[]{:S(2)}) copy-start(s32[32,512]{1,0:T(8,128)} %param.14) | copy-start | bytes 196612
  3.5 10.4 %copy-start.7 = (s32[32,512]{1,0:T(8,128)S(1)}, s32[32,512]{1,0:T(8,128)}, u32[]{:S(2)}) copy-start(s32[32,512]{1,0:T(8,128)} %param.13) | copy-start | bytes 196612
  5.8 10.2 %copy-start.8 = (s32[512]{0:T(512)S(1)}, s32[512]{0:T(512)}, u32[]{:S(2)}) copy-start(s32[512]{0:T(512)} %param.17) | copy-start | bytes 6148
  13.7 2.6 %copy-start.2 = (bf16[256,256]{1,0:T(8,128)(2,1)S(1)}, bf16[256,256]{1,0:T(8,128)(2,1)}, u32[]{:S(2)}) copy-start(bf16[256,256]{1,0:T(8,128)(2,1)} %constant.47.focus_ref) | copy-start | bytes 393220
  13.7 2.6 %copy-start.5 = (s32[32]{0:T(128)S(1)}, s32[32]{0:T(128)}, u32[]{:S(2)}) copy-start(s32[32]{0:T(128)} %rate_ref.1) | copy-start | bytes 388

commit v2 on v0

v2 whole, which is shorter than its diff:
```python
import math

import ml_dtypes
import numpy as np
import jax
import jax.numpy as jnp
from jax import lax
from jax.experimental import pallas as pl
from jax.experimental.pallas import tpu as pltpu
from jax.sharding import PartitionSpec as P

MESH = pl.DeviceIdType.MESH
F32 = jnp.float32
BF16 = jnp.bfloat16
TWO_PI = 2.0 * math.pi
PIECES = [(slice(r, r + 16), slice(c, c + 512)) for r in (0, 16) for c in (0, 512)]


def dft_tables():
    k, i = np.arange(64)[:, None], np.arange(64)[None, :]
    a = TWO_PI * (k * i % 64) / 64
    c, s = np.cos(a), np.sin(a)
    first = np.kron(np.block([[c, s], [-s, c]]), np.eye(8)).astype(ml_dtypes.bfloat16)
    bins = np.arange(128)[None, :]
    t = TWO_PI * (k * bins % 8192) / 8192
    twist = np.stack([np.cos(t), -np.sin(t)]).astype(np.float32)
    v = np.arange(128)[:, None]
    b = TWO_PI * (v * bins % 128) / 128
    c, s = np.cos(b), np.sin(b)
    order = np.concatenate([np.arange(0, 128, 2), np.arange(1, 128, 2)])
    second = np.concatenate([c[order], s[order]], axis=1).astype(ml_dtypes.bfloat16)
    focus = np.block([[c, s], [-s, c]]).astype(ml_dtypes.bfloat16)
    return first, twist, second, focus


def swap_bits(blocks, low):
    blocks = list(blocks)
    lane = lax.broadcasted_iota(jnp.int32, blocks[0].shape, 1)
    bit = 1
    while bit < len(blocks):
        shift = bit << low
        high = (lane & shift) != 0
        for i in range(len(blocks)):
            if i & bit == 0:
                a, b = blocks[i], blocks[i | bit]
                blocks[i] = jnp.where(high, pltpu.roll(b, shift, 1), a)
                blocks[i | bit] = jnp.where(high, b, pltpu.roll(a, 128 - shift, 1))
        bit *= 2
    return blocks


def unit_root(x):
    x = x - jnp.where(x >= 0.5, 1.0, 0.0)
    h = x * math.pi
    q = h * h
    sh = h * (1.0 + q * (-1 / 6 + q * (1 / 120 + q * (-1 / 5040 + q * (1 / 362880)))))
    ch = 1.0 + q * (-1 / 2 + q * (1 / 24 + q * (-1 / 720 + q * (1 / 40320 + q * (-1 / 3628800)))))
    return 1.0 - 2.0 * sh * sh, 2.0 * sh * ch


def distance(d):
    hops = [0, 1, 2, 1]
    return hops[(d >> 3) & 3] + hops[(d >> 1) & 3] + (d >> 5) + 0.3 * (d & 1)


PEERS = sorted(range(1, 64), key=lambda d: -distance(d))


def image_kernel(
    rate_ref, error_ref, raw_ref, taper_ref, offset_ref, seen_ref, group_ref,
    first_ref, twist_ref, second_ref, focus_ref, out_ref,
    signal, mid, terms, msg, recv, pick, gath, weight, phase, part_a, part_b,
    send_a, send_b, recv_a, recv_b, msg2, recv2,
    sem_s1, sem_r1, sem_sa, sem_ra, sem_sb, sem_rb, sem_s2, sem_r2,
):
    py = lax.axis_index("pulse")
    zc = lax.axis_index("tile")
    wx = lax.axis_index("row")
    core, zb, zp = zc & 1, (zc >> 1) & 1, zc >> 2

    def peer(d):
        p, w = (py + ((d >> 3) & 3)) & 3, (wx + ((d >> 1) & 3)) & 3
        b, c = zb ^ (d >> 5), core ^ (d & 1)
        return (p, zp * 4 + b * 2 + c, w), b * 32 + p * 8 + w * 2 + c, p * 8 + w * 2 + b

    me = zb * 32 + py * 8 + wx * 2 + core
    own_slot = (((py & 1) * 4 + wx) * 4 + zb * 2 + core) * 2 + (py >> 1)
    up = (py, (zc + 4) & 31, wx)
    down = (py, (zc + 28) & 31, wx)

    barrier = pltpu.get_barrier_semaphore()
    for d in PEERS:
        pl.semaphore_signal(barrier, inc=1, device_id=peer(d)[0], device_id_type=MESH)
    pl.semaphore_signal(barrier, inc=1, device_id=up, device_id_type=MESH)
    pl.semaphore_signal(barrier, inc=1, device_id=down, device_id_type=MESH)

    for ri in range(2):
        for i in range(0, 64, 2):
            halves = []
            for jh in range(2):
                pair = [
                    raw_ref[ri, jh * 8:jh * 8 + 8, n * 128:n * 128 + 128] * taper_ref[n:n + 1, :]
                    for n in (i, i + 1)
                ]
                halves.append(jnp.concatenate(pair, axis=0).astype(BF16))
            at = (ri * 64 + i) * 8
            signal[at:at + 16, 0:128] = halves[0]
            signal[at:at + 16, 128:256] = halves[1]
    mid[...] = jnp.dot(first_ref[...], signal[...], preferred_element_type=F32)

    def turn(k, carry):
        y_re = mid[pl.ds(pl.multiple_of(k * 8, 8), 8), :]
        y_im = mid[pl.ds(pl.multiple_of(512 + k * 8, 8), 8), :]
        t_re, t_im = twist_ref[0, pl.ds(k, 1), :], twist_ref[1, pl.ds(k, 1), :]
        res, ims = [], []
        for jh in range(2):
            a, b = y_re[:, jh * 128:jh * 128 + 128], y_im[:, jh * 128:jh * 128 + 128]
            res.append(a * t_re - b * t_im)
            ims.append(a * t_im + b * t_re)
        b_re, b_im = jnp.concatenate(res, axis=0), jnp.concatenate(ims, axis=0)
        at = pl.multiple_of(k * 32, 32)
        terms[pl.ds(at, 16), 0:128] = b_re.astype(BF16)
        terms[pl.ds(at, 16), 128:256] = b_im.astype(BF16)
        terms[pl.ds(at + 16, 16), 0:128] = b_im.astype(BF16)
        terms[pl.ds(at + 16, 16), 128:256] = (-b_re).astype(BF16)
        return carry

    lax.fori_loop(0, 64, turn, 0, unroll=4)

    def spectrum(n, carry):
        rows = terms[pl.ds(pl.multiple_of(n * 256, 256), 256), :]
        x = lax.dot_general(
            second_ref[...], rows, (((1,), (1,)), ((), ())), preferred_element_type=F32
        ) * (1.0 / math.sqrt(8192))
        for g in range(2):
            blocks = swap_bits([x[a * 32:a * 32 + 32, g * 128:g * 128 + 128] for a in range(4)], 5)
            for i in range(4):
                msg[n * 8 + g * 4 + i] = blocks[i].astype(BF16)
        return carry

    lax.fori_loop(0, 8, spectrum, 0)

    pl.semaphore_wait(barrier, 65)

    for d in PEERS:
        where, index, _ = peer(d)
        pltpu.make_async_remote_copy(
            src_ref=msg.at[index], dst_ref=recv.at[own_slot], send_sem=sem_s1.at[0], recv_sem=sem_r1.at[0],
            device_id=where, device_id_type=MESH,
        ).start()
    all_first = pltpu.make_async_remote_copy(
        src_ref=msg.at[pl.ds(0, 63)], dst_ref=recv.at[pl.ds(0, 63)], send_sem=sem_s1.at[0], recv_sem=sem_r1.at[0],
        device_id=peer(1)[0], device_id_type=MESH,
    )
    recv[own_slot] = msg[me]

    def azimuth(t, carry):
        rate = rate_ref[t]
        low = lax.broadcasted_iota(jnp.int32, (8, 512), 0)
        row = lax.broadcasted_iota(jnp.int32, (8, 512), 1)
        step = (low * rate) & 4095
        a_re, a_im = unit_root(((step * row) & 4095).astype(F32) * (1 / 4096))
        b_re, b_im = unit_root(((((step * 8) & 4095) * row) & 4095).astype(F32) * (1 / 4096))
        for w in range(4):
            parts_re, parts_im = [], []
            for k in (2 * w, 2 * w + 1):
                k_re, k_im = b_re[k:k + 1, :], b_im[k:k + 1, :]
                parts_re.append(a_re * k_re - a_im * k_im)
                parts_im.append(a_re * k_im + a_im * k_re)
            e_re = jnp.concatenate(parts_re, axis=0)
            e_im = jnp.concatenate(parts_im, axis=0)
            weight[t, w * 32:w * 32 + 16, 0:512] = e_re.astype(BF16)
            weight[t, w * 32:w * 32 + 16, 512:1024] = e_im.astype(BF16)
            weight[t, w * 32 + 16:w * 32 + 32, 0:512] = (-e_im).astype(BF16)
            weight[t, w * 32 + 16:w * 32 + 32, 512:1024] = e_re.astype(BF16)
        sub = lax.broadcasted_iota(jnp.int32, (16, 128), 0)
        lane = lax.broadcasted_iota(jnp.int32, (16, 128), 1)
        for p2 in range(2):
            sigma = p2 * 32 + zp * 4 + sub // 4
            s_re, s_im = unit_root(((((sigma * rate) & 63) * lane) & 63).astype(F32) * (1 / 64))
            phase[t, 2 * p2] = s_re
            phase[t, 2 * p2 + 1] = s_im
        return carry

    lax.fori_loop(0, 32, azimuth, 0)

    starts = jnp.where(seen_ref[...] != 0, offset_ref[...], -64).astype(F32).astype(BF16)
    sub = lax.broadcasted_iota(jnp.int32, (16, 256), 0)
    lane = lax.broadcasted_iota(jnp.int32, (16, 256), 1)
    unit = jnp.where((sub >> 2) == (lane >> 6), (lane & 31) - (sub & 3), 1000).astype(F32)

    def choose(n, carry):
        block = lax.broadcasted_iota(jnp.int32, (512, 256), 0)
        col = lax.broadcasted_iota(jnp.int32, (512, 256), 1)
        h, ss = (col >> 5) & 1, col >> 6
        here = (2 * h + (n >> 2)) * 128 + zp * 16 + ss * 4 + (n & 3)
        place = jnp.dot(starts, jnp.where(block == here, 1.0, 0.0).astype(BF16), preferred_element_type=F32)
        for t in range(32):
            line = place[t:t + 1, :]
            for uh in range(2):
                pick[n, uh, t * 16:t * 16 + 16, :] = jnp.where(line == unit + 32.0 * uh, 1.0, 0.0).astype(BF16)
        return carry

    lax.fori_loop(0, 8, choose, 0)

    all_first.wait_recv()

    def gather(n, carry):
        p2, part = n >> 2, n & 3
        rows = pl.ds(pl.multiple_of(part * 128, 128), 128)
        odd = (lax.broadcasted_iota(jnp.int32, (16, 128), 1) & 32) != 0
        found = []
        for w in range(4):
            data = recv[pl.ds(pl.multiple_of((p2 * 4 + w) * 8, 8), 8)].reshape(256, 128)
            found.append([
                jnp.dot(pick[p2 * 4 + w, uh, rows, :], data, preferred_element_type=F32) for uh in range(2)
            ])
        for i in range(8):
            m = [jnp.where(odd, f[1][i * 16:i * 16 + 16], f[0][i * 16:i * 16 + 16]) for f in found]
            pairs = [
                jnp.where(odd, m[k + 1] + pltpu.roll(m[k + 1], 32, 1), m[k] + pltpu.roll(m[k], 96, 1))
                for k in (0, 2)
            ]
            pairs = swap_bits(pairs, 6)
            for vi in range(2):
                gath[part * 8 + i, pl.ds(pl.multiple_of((vi * 2 + p2) * 16, 16), 16), :] = pairs[vi].astype(BF16)
        return carry

    lax.fori_loop(0, 8, gather, 0)

    def partial_image(dest, store):
        top = lax.broadcasted_iota(jnp.int32, (8, 128), 0) < 4
        for pair in range(2):
            sums = []
            for k in range(2):
                t = dest * 4 + pair * 2 + k
                y = jnp.dot(gath[t], weight[t], preferred_element_type=F32)
                s = [phase[t, i] for i in range(4)]
                mine = {}
                for g in range(4):
                    for vi in range(2):
                        tot_re = tot_im = None
                        for p2 in range(2):
                            rows = slice((vi * 2 + p2) * 16, (vi * 2 + p2) * 16 + 16)
                            y_re = y[rows, g * 128:g * 128 + 128]
                            y_im = y[rows, 512 + g * 128:640 + g * 128]
                            r = y_re * s[2 * p2] - y_im * s[2 * p2 + 1]
                            i = y_re * s[2 * p2 + 1] + y_im * s[2 * p2]
                            tot_re = r if tot_re is None else tot_re + r
                            tot_im = i if tot_im is None else tot_im + i
                        for ri, tot in ((0, tot_re), (1, tot_im)):
                            tot = tot[:8] + tot[8:]
                            mine[ri, g, vi] = tot + pltpu.roll(tot, 4, 0)
                sums.append(mine)
            for ri in range(2):
                for g in range(4):
                    for vi in range(2):
                        both = jnp.where(top, sums[0][ri, g, vi], sums[1][ri, g, vi])
                        row, at = vi * 16 + pair * 8, ri * 512 + g * 128
                        store[row:row + 8, at:at + 128] = both

    def ring_copy(src, dst, send_sem, recv_sem, step, h, where):
        rows, lanes = PIECES[h]
        return pltpu.make_async_remote_copy(
            src_ref=src.at[step, rows, lanes], dst_ref=dst.at[step, rows, lanes],
            send_sem=send_sem.at[step, h], recv_sem=recv_sem.at[step, h],
            device_id=where, device_id_type=MESH,
        )

    def copy_a(step, h):
        return ring_copy(send_a, recv_a, sem_sa, sem_ra, step, h, up)

    def copy_b(step, h):
        return ring_copy(send_b, recv_b, sem_sb, sem_rb, step, h, down)

    partial_image((zp + 4) & 7, part_a)
    for h in range(4):
        rows, lanes = PIECES[h]
        send, copy = (send_a, copy_a) if h < 2 else (send_b, copy_b)
        send[0, rows, lanes] = part_a[rows, lanes].astype(BF16)
        copy(0, h).start()
    for s in range(1, 4):
        partial_image((zp + 4 - s) & 7, part_a)
        partial_image((zp + 4 + s) & 7, part_b)
        for h in range(4):
            rows, lanes = PIECES[h]
            for part, send, got, copy, late in (
                (part_a, send_a, recv_a, copy_a, h < 2), (part_b, send_b, recv_b, copy_b, h >= 2)
            ):
                total = part[rows, lanes]
                if s > 1 or late:
                    copy(s - 1, h).wait_recv()
                    total = total + got[s - 1, rows, lanes].astype(F32)
                send[s, rows, lanes] = total.astype(BF16)
                copy(s, h).start()
    partial_image(zp, part_a)

    top = lax.broadcasted_iota(jnp.int32, (8, 128), 0) < 4
    turns = {}
    for q in range(4):
        labels = jnp.broadcast_to(group_ref[q:q + 1, :], (8, 128))
        for pair in range(2):
            angle = jnp.zeros((8, 128), F32)
            t = zp * 4 + pair * 2
            for n in range(16):
                angle = jnp.where(labels == n, jnp.where(top, error_ref[t, n], error_ref[t + 1, n]), angle)
            turns[q, pair] = unit_root(angle * (1.0 / TWO_PI))

    for h in range(4):
        rows, lanes = PIECES[h]
        copy_a(3, h).wait_recv()
        copy_b(3, h).wait_recv()
        part_a[rows, lanes] = (
            part_a[rows, lanes] + recv_a[3, rows, lanes].astype(F32) + recv_b[3, rows, lanes].astype(F32)
        )

    rights = []
    for vi in range(2):
        for q in range(4):
            for pair in range(2):
                row, at = vi * 16 + pair * 8, q * 128
                i_re = part_a[row:row + 8, at:at + 128]
                i_im = part_a[row:row + 8, 512 + at:640 + at]
                c, s = turns[q, pair]
                rights.append(jnp.concatenate([i_re * c - i_im * s, i_re * s + i_im * c], axis=1))
    right = (jnp.concatenate(rights, axis=0) * (1.0 / 1024)).astype(BF16)
    spun = lax.dot_general(focus_ref[...], right, (((1,), (1,)), ((), ())), preferred_element_type=F32)
    for w in range(4):
        blocks = []
        for i in range(8):
            at = (i // 4) * 128 + w * 32 + (i % 4) * 8
            blocks.append(spun[at:at + 8, :])
        blocks = swap_bits(blocks, 3)
        for i in range(8):
            msg2[(i // 2) * 8 + w * 2 + i % 2] = blocks[i]

    for d in PEERS:
        where, _, index = peer(d)
        pltpu.make_async_remote_copy(
            src_ref=msg2.at[index], dst_ref=recv2.at[me], send_sem=sem_s2.at[0], recv_sem=sem_r2.at[0],
            device_id=where, device_id_type=MESH,
        ).start()
    recv2[me] = msg2[py * 8 + wx * 2 + zb]

    all_first.wait_send()
    for s in range(4):
        for h in range(4):
            if s > 0 or h < 2:
                copy_a(s, h).wait_send()
            if s > 0 or h >= 2:
                copy_b(s, h).wait_send()
    all_last = pltpu.make_async_remote_copy(
        src_ref=recv2.at[pl.ds(0, 63)], dst_ref=recv2.at[pl.ds(0, 63)], send_sem=sem_s2.at[0], recv_sem=sem_r2.at[0],
        device_id=peer(1)[0], device_id_type=MESH,
    )
    all_last.wait_recv()

    high = (lax.broadcasted_iota(jnp.int32, (8, 128), 1) & 4) != 0
    blocks = []
    for n in range(32):
        k = (n >> 2) * 8 + (n & 3)
        a, b = recv2[k], recv2[k + 4]
        even = jnp.where(high, pltpu.roll(b, 4, 1), a)
        odd = jnp.where(high, b, pltpu.roll(a, 124, 1))
        blocks.append(jnp.where(core == 0, even, odd))
    low = swap_bits_of(blocks, ((1, 1), (2, 2), (4, 8), (8, 16), (16, 32)))
    for i in range(32):
        ri, hi, unit_at = i // 16, (i // 4) % 4, i % 4
        at = ri * 512 + unit_at * 128
        out_ref[hi * 8:hi * 8 + 8, at:at + 128] = low[i]
    all_last.wait_send()


def swap_bits_of(blocks, pairs):
    blocks = list(blocks)
    lane = lax.broadcasted_iota(jnp.int32, blocks[0].shape, 1)
    for bit, shift in pairs:
        high = (lane & shift) != 0
        for i in range(len(blocks)):
            if i & bit == 0:
                a, b = blocks[i], blocks[i | bit]
                blocks[i] = jnp.where(high, pltpu.roll(b, shift, 1), a)
                blocks[i | bit] = jnp.where(high, b, pltpu.roll(a, 128 - shift, 1))
    return blocks


def body(raw_pulses, range_weight, visibility, offsets, doppler_rate, phase_error, row_groups):
    first, twist, second, focus = dft_tables()
    vmem = pl.BlockSpec(memory_space=pltpu.VMEM)
    smem = pl.BlockSpec(memory_space=pltpu.SMEM)
    dma = pltpu.SemaphoreType.DMA
    focused = pl.pallas_call(
        image_kernel,
        out_shape=jax.ShapeDtypeStruct((32, 1024), F32),
        in_specs=[smem, smem] + [vmem] * 9,
        out_specs=vmem,
        scratch_shapes=[
            pltpu.VMEM((1024, 256), BF16),
            pltpu.VMEM((1024, 256), F32),
            pltpu.VMEM((2048, 256), BF16),
            pltpu.VMEM((64, 32, 128), BF16),
            pltpu.VMEM((64, 32, 128), BF16),
            pltpu.VMEM((8, 2, 512, 256), BF16),
            pltpu.VMEM((32, 64, 128), BF16),
            pltpu.VMEM((32, 128, 1024), BF16),
            pltpu.VMEM((32, 4, 16, 128), F32),
            pltpu.VMEM((32, 1024), F32),
            pltpu.VMEM((32, 1024), F32),
            pltpu.VMEM((4, 32, 1024), BF16),
            pltpu.VMEM((4, 32, 1024), BF16),
            pltpu.VMEM((4, 32, 1024), BF16),
            pltpu.VMEM((4, 32, 1024), BF16),
            pltpu.VMEM((32, 8, 128), F32),
            pltpu.VMEM((64, 8, 128), F32),
            dma((1,)), dma((1,)),
            dma((4, 4)), dma((4, 4)), dma((4, 4)), dma((4, 4)),
            dma((1,)), dma((1,)),
        ],
        compiler_params=pltpu.CompilerParams(
            collective_id=0, has_side_effects=True, vmem_limit_bytes=48 * 2**20
        ),
    )(
        doppler_rate, phase_error, raw_pulses, range_weight.reshape(64, 128), offsets, visibility,
        row_groups.reshape(4, 128), jnp.asarray(first), jnp.asarray(twist), jnp.asarray(second), jnp.asarray(focus),
    )
    return focused[None]


def solution(mesh):
    return jax.shard_map(
        body,
        mesh=mesh,
        in_specs=(P(None, ("pulse", "tile", "row"), None), P(), P(), P(), P(), P(), P()),
        out_specs=P("tile", ("pulse", "row"), None),
        check_vma=False,
    )
```

time: 280 us -> 64.8 us (0.23); the launches traced: 276 us -> 64.3 us
  waiting for transfers between devices: 127 us -> 0 us
  local copies, waits for them, and re-layouts: 90.4 us -> 10.6 us
  Pallas kernels: 0 us -> 53.7 us
  starting transfers between devices: 16.9 us -> 0 us
  between operations: 13.6 us -> 0.02 us
  blocking collectives: 9.57 us -> 0 us
  matrix products: 9.05 us -> 0 us
  other arithmetic: 9.01 us -> 0 us
    gather x192 -> x0, local copies, waits for them, and re-layouts: 83.8 us -> none
    reduce_scatter x1 -> x0, waiting for transfers between devices: 77.4 us -> none  [body(): lax.psum_scatter((summed * norm_factor).astype(jnp.bfloat16), ('pulse', '...]
    pallas_call x0 -> x1, Pallas kernels: none -> 53.7 us  [body(): pl.pallas_call(image_kernel, out_shape=jax.ShapeDtypeStruct((32, 1024), F...]
    all_to_all x1 -> x0, waiting for transfers between devices: 49.5 us -> none  [body(): lax.all_to_all(as_sent(windows), 'tile', split_axis=0, concat_axis=0, til...]
    all_to_all x1 -> x0, starting transfers between devices: 16.9 us -> none  [body(): lax.all_to_all(as_sent(windows), 'tile', split_axis=0, concat_axis=0, til...]
    all_gather x1 -> x0, blocking collectives: 9.57 us -> none  [body(): lax.all_gather(image_share, 'row', axis=0, tiled=True).astype(jnp.float32)]
    dot_general x14 -> x0, matrix products: 9.05 us -> none  [the longest x2 1.58 us: complex_einsum(): product(left_im, right_im)]
    unnamed x15 -> x22, local copies, waits for them, and re-layouts: 3.52 us -> 10.6 us
  transfers between devices with their start and end apart: 2 -> 0, of which waited for: 2 -> 0; matrix products, arithmetic and copies ran while one was open for 3% -> 0% of each run, Pallas kernels for 0% -> 0%
where the time goes in v2:
time: 64.8 us; the launch traced here: 64.3 us
  Pallas kernels  53.7 us (83%)
  local copies, waits for them, and re-layouts  10.6 us (16%)
    pallas_call x1, Pallas kernels, body(): pl.pallas_call(image_kernel, out_shape=jax.ShapeDtypeStruct((32, 1024), F...  53.7 us
    unnamed x22, local copies, waits for them, and re-layouts  10.6 us

profile of v2, /device:TPU:1, one launch (start us, length us, event | category | flops | bytes accessed | tf_op | source)
XLA Modules:
  0.0 64.3 jit_solution(4510679782248919708)
XLA Ops:
  0.0 0.8 %copy.12.error_ref = f32[32,16]{1,0:T(8,128)S(1)} copy(f32[32,16]{0,1:T(8,128)} %param.16) | data formatting | bytes 4096 | tf_op args[5]
  0.8 0.0 copy-start
  0.8 1.6 %copy-done = bf16[1024,1024]{1,0:T(8,128)(2,1)S(1)} copy-done((bf16[1024,1024]{1,0:T(8,128)(2,1)S(1)}, bf16[1024,1024]{1,0:T(8,128)(2,1)}, u32[]{:S(2)}) %copy-start) | copy-done | bytes 2097176
  2.4 0.0 copy-start.1
  2.4 1.2 %copy-done.1 = f32[2,16,8192]{2,1,0:T(8,128)S(1)} copy-done((f32[2,16,8192]{2,1,0:T(8,128)S(1)}, f32[2,16,8192]{2,1,0:T(8,128)}, u32[]{:S(2)}) %copy-start.1) | copy-done | bytes 1048600
  3.6 0.0 copy-start.2
  3.6 0.9 %copy-done.2 = bf16[256,256]{1,0:T(8,128)(2,1)S(1)} copy-done((bf16[256,256]{1,0:T(8,128)(2,1)S(1)}, bf16[256,256]{1,0:T(8,128)(2,1)}, u32[]{:S(2)}) %copy-start.2) | copy-done | bytes 131096
  4.5 0.0 copy-start.3
  4.5 0.8 %copy-done.3 = s32[32,512]{1,0:T(8,128)S(1)} copy-done((s32[32,512]{1,0:T(8,128)S(1)}, s32[32,512]{1,0:T(8,128)}, u32[]{:S(2)}) %copy-start.3) | copy-done | bytes 65560
  5.3 0.0 copy-start.4
  5.3 0.8 %copy-done.4 = s32[32,512]{1,0:T(8,128)S(1)} copy-done((s32[32,512]{1,0:T(8,128)S(1)}, s32[32,512]{1,0:T(8,128)}, u32[]{:S(2)}) %copy-start.4) | copy-done | bytes 65560
  6.2 0.0 copy-start.5
  6.2 0.8 %copy-done.5 = bf16[128,256]{1,0:T(8,128)(2,1)S(1)} copy-done((bf16[128,256]{1,0:T(8,128)(2,1)S(1)}, bf16[128,256]{1,0:T(8,128)(2,1)}, u32[]{:S(2)}) %copy-start.5) | copy-done | bytes 65560
  7.0 0.0 copy-start.6
  7.0 0.8 %copy-done.6 = f32[2,64,128]{2,1,0:T(8,128)S(1)} copy-done((f32[2,64,128]{2,1,0:T(8,128)S(1)}, f32[2,64,128]{2,1,0:T(8,128)}, u32[]{:S(2)}) %copy-start.6) | copy-done | bytes 65560
  7.9 0.0 copy-start.7
  7.9 0.8 %copy-done.7 = f32[8192]{0:T(1024)S(1)} copy-done((f32[8192]{0:T(1024)S(1)}, f32[8192]{0:T(1024)}, u32[]{:S(2)}) %copy-start.7) | copy-done | bytes 32792
  8.6 0.0 copy-start.8
  8.6 0.7 %copy-done.8 = s32[512]{0:T(512)S(1)} copy-done((s32[512]{0:T(512)S(1)}, s32[512]{0:T(512)}, u32[]{:S(2)}) %copy-start.8) | copy-done | bytes 2072
  9.3 0.0 copy-start.9
  9.3 0.7 %copy-done.9 = s32[32]{0:T(128)S(1)} copy-done((s32[32]{0:T(128)S(1)}, s32[32]{0:T(128)}, u32[]{:S(2)}) %copy-start.9) | copy-done | bytes 152
  9.9 53.7 %shard_map.109 = f32[32,1024]{1,0:T(8,128)S(1)} custom-call(s32[32]{0:T(128)S(1)} %copy-done.9, f32[32,16]{1,0:T(8,128)S(1)} %copy.12.error_ref, f32[2,16,8192]{2,1,0:T(8,128)S(1)} %copy-done.1, f32[64,128]{1,0:T(8,128)S(1)} %bitcast.4, s32[32,512]{1,0:T(8,128)S(1)} %copy-done.3, s32[32,512]{1,0:T(8,128)S(1)} %copy-done.4, s32[4,128]{1,0:T(4,128)S(1)} %bitcast.5, ...), custom_call_target="tpu_custom_call" | custom-call | tf_op jit(solution)/shard_map/pallas_call | solution.py:392
  63.7 0.7 %copy.14 = f32[1,32,1024]{2,1,0:T(8,128)} copy(f32[1,32,1024]{2,1,0:T(8,128)S(1)} %bitcast.3) | data formatting | bytes 262144
Async XLA Ops:
  0.8 1.6 %copy-start = (bf16[1024,1024]{1,0:T(8,128)(2,1)S(1)}, bf16[1024,1024]{1,0:T(8,128)(2,1)}, u32[]{:S(2)}) copy-start(bf16[1024,1024]{1,0:T(8,128)(2,1)} %constant.8.clone.first_ref) | copy-start | bytes 6291460
  2.4 1.2 %copy-start.1 = (f32[2,16,8192]{2,1,0:T(8,128)S(1)}, f32[2,16,8192]{2,1,0:T(8,128)}, u32[]{:S(2)}) copy-start(f32[2,16,8192]{2,1,0:T(8,128)} %raw_ref.1) | copy-start | bytes 3145732
  3.6 0.9 %copy-start.2 = (bf16[256,256]{1,0:T(8,128)(2,1)S(1)}, bf16[256,256]{1,0:T(8,128)(2,1)}, u32[]{:S(2)}) copy-start(bf16[256,256]{1,0:T(8,128)(2,1)} %constant.11.clone.focus_ref) | copy-start | bytes 393220
  4.5 0.8 %copy-start.3 = (s32[32,512]{1,0:T(8,128)S(1)}, s32[32,512]{1,0:T(8,128)}, u32[]{:S(2)}) copy-start(s32[32,512]{1,0:T(8,128)} %offset_ref.1) | copy-start | bytes 196612
  5.3 0.8 %copy-start.4 = (s32[32,512]{1,0:T(8,128)S(1)}, s32[32,512]{1,0:T(8,128)}, u32[]{:S(2)}) copy-start(s32[32,512]{1,0:T(8,128)} %seen_ref.1) | copy-start | bytes 196612
  6.2 0.8 %copy-start.5 = (bf16[128,256]{1,0:T(8,128)(2,1)S(1)}, bf16[128,256]{1,0:T(8,128)(2,1)}, u32[]{:S(2)}) copy-start(bf16[128,256]{1,0:T(8,128)(2,1)} %constant.10.clone.second_ref) | copy-start | bytes 196612
  7.0 0.8 %copy-start.6 = (f32[2,64,128]{2,1,0:T(8,128)S(1)}, f32[2,64,128]{2,1,0:T(8,128)}, u32[]{:S(2)}) copy-start(f32[2,64,128]{2,1,0:T(8,128)} %constant.9.clone.twist_ref) | copy-start | bytes 196612
  7.9 0.8 %copy-start.7 = (f32[8192]{0:T(1024)S(1)}, f32[8192]{0:T(1024)}, u32[]{:S(2)}) copy-start(f32[8192]{0:T(1024)} %param.12) | copy-start | bytes 98308
  8.6 0.7 %copy-start.8 = (s32[512]{0:T(512)S(1)}, s32[512]{0:T(512)}, u32[]{:S(2)}) copy-start(s32[512]{0:T(512)} %param.17) | copy-start | bytes 6148
  9.3 0.7 %copy-start.9 = (s32[32]{0:T(128)S(1)}, s32[32]{0:T(128)}, u32[]{:S(2)}) copy-start(s32[32]{0:T(128)} %rate_ref.1) | copy-start | bytes 388

commit v3 on v2

--- a/solution.py
+++ b/solution.py
@@ -64,11 +64,14 @@
 
 
 PEERS = sorted(range(1, 64), key=lambda d: -distance(d))
+PEERS_BY_PARITY = [d for d in PEERS if (d >> 3) & 1 == 0] + [d for d in PEERS if (d >> 3) & 1 == 1]
 
 
 def image_kernel(
+    rate_in, error_in, raw_in, taper_in, offset_in, seen_in, group_in,
+    first_in, twist_in, second_in, focus_in, out_ref,
     rate_ref, error_ref, raw_ref, taper_ref, offset_ref, seen_ref, group_ref,
-    first_ref, twist_ref, second_ref, focus_ref, out_ref,
+    first_ref, twist_ref, second_ref, focus_ref, sem_in,
     signal, mid, terms, msg, recv, pick, gath, weight, phase, part_a, part_b,
     send_a, send_b, recv_a, recv_b, msg2, recv2,
     sem_s1, sem_r1, sem_sa, sem_ra, sem_sb, sem_rb, sem_s2, sem_r2,
@@ -88,12 +91,25 @@
     up = (py, (zc + 4) & 31, wx)
     down = (py, (zc + 28) & 31, wx)
 
+    loads = [
+        pltpu.make_async_copy(a, b, sem_in.at[i])
+        for i, (a, b) in enumerate((
+            (raw_in, raw_ref), (first_in, first_ref), (taper_in, taper_ref), (twist_in, twist_ref),
+            (second_in, second_ref), (rate_in, rate_ref), (offset_in, offset_ref), (seen_in, seen_ref),
+            (error_in, error_ref), (group_in, group_ref), (focus_in, focus_ref),
+        ))
+    ]
+    for load in loads:
+        load.start()
+
     barrier = pltpu.get_barrier_semaphore()
     for d in PEERS:
         pl.semaphore_signal(barrier, inc=1, device_id=peer(d)[0], device_id_type=MESH)
     pl.semaphore_signal(barrier, inc=1, device_id=up, device_id_type=MESH)
     pl.semaphore_signal(barrier, inc=1, device_id=down, device_id_type=MESH)
 
+    for i in (0, 2):
+        loads[i].wait()
     for ri in range(2):
         for i in range(0, 64, 2):
             halves = []
@@ -106,7 +122,11 @@
             at = (ri * 64 + i) * 8
             signal[at:at + 16, 0:128] = halves[0]
             signal[at:at + 16, 128:256] = halves[1]
+    loads[1].wait()
     mid[...] = jnp.dot(first_ref[...], signal[...], preferred_element_type=F32)
+
+    for i in (3, 4):
+        loads[i].wait()
 
     def turn(k, carry):
         y_re = mid[pl.ds(pl.multiple_of(k * 8, 8), 8), :]
@@ -142,17 +162,28 @@
 
     pl.semaphore_wait(barrier, 65)
 
-    for d in PEERS:
+    parity = py & 1
+    for d in PEERS_BY_PARITY:
         where, index, _ = peer(d)
         pltpu.make_async_remote_copy(
-            src_ref=msg.at[index], dst_ref=recv.at[own_slot], send_sem=sem_s1.at[0], recv_sem=sem_r1.at[0],
+            src_ref=msg.at[index], dst_ref=recv.at[own_slot], send_sem=sem_s1.at[0], recv_sem=sem_r1.at[parity],
             device_id=where, device_id_type=MESH,
         ).start()
     all_first = pltpu.make_async_remote_copy(
         src_ref=msg.at[pl.ds(0, 63)], dst_ref=recv.at[pl.ds(0, 63)], send_sem=sem_s1.at[0], recv_sem=sem_r1.at[0],
         device_id=peer(1)[0], device_id_type=MESH,
     )
-    recv[own_slot] = msg[me]
+    pltpu.make_async_copy(msg.at[me], recv.at[own_slot], sem_r1.at[parity]).start()
+
+    def half_first(p2):
+        half = pl.ds(pl.multiple_of(p2 * 32, 32), 32)
+        return pltpu.make_async_remote_copy(
+            src_ref=msg.at[pl.ds(0, 32)], dst_ref=recv.at[half], send_sem=sem_s1.at[0], recv_sem=sem_r1.at[p2],
+            device_id=peer(1)[0], device_id_type=MESH,
+        )
+
+    for load in loads[5:]:
+        load.wait()
 
     def azimuth(t, carry):
         rate = rate_ref[t]
@@ -203,10 +234,7 @@
 
     lax.fori_loop(0, 8, choose, 0)
 
-    all_first.wait_recv()
-
-    def gather(n, carry):
-        p2, part = n >> 2, n & 3
+    def gather(p2, part):
         rows = pl.ds(pl.multiple_of(part * 128, 128), 128)
         odd = (lax.broadcasted_iota(jnp.int32, (16, 128), 1) & 32) != 0
         found = []
@@ -224,9 +252,20 @@
             pairs = swap_bits(pairs, 6)
             for vi in range(2):
                 gath[part * 8 + i, pl.ds(pl.multiple_of((vi * 2 + p2) * 16, 16), 16), :] = pairs[vi].astype(BF16)
-        return carry
-
-    lax.fori_loop(0, 8, gather, 0)
+
+    def gather_early(part, carry):
+        gather(parity, part)
+        return carry
+
+    def gather_late(part, carry):
+        gather(1 - parity, (far + part) & 3)
+        return carry
+
+    far = ((zp + 4) & 7) >> 1
+    half_first(parity).wait_recv()
+    lax.fori_loop(0, 4, gather_early, 0)
+    half_first(1 - parity).wait_recv()
+    gather(1 - parity, far)
 
     def partial_image(dest, store):
         top = lax.broadcasted_iota(jnp.int32, (8, 128), 0) < 4
@@ -279,6 +318,7 @@
         send, copy = (send_a, copy_a) if h < 2 else (send_b, copy_b)
         send[0, rows, lanes] = part_a[rows, lanes].astype(BF16)
         copy(0, h).start()
+    lax.fori_loop(1, 4, gather_late, 0)
     for s in range(1, 4):
         partial_image((zp + 4 - s) & 7, part_a)
         partial_image((zp + 4 + s) & 7, part_b)
@@ -303,7 +343,7 @@
             angle = jnp.zeros((8, 128), F32)
             t = zp * 4 + pair * 2
             for n in range(16):
-                angle = jnp.where(labels == n, jnp.where(top, error_ref[t, n], error_ref[t + 1, n]), angle)
+                angle = jnp.where(labels == n, jnp.where(top, error_ref[n, t], error_ref[n, t + 1]), angle)
             turns[q, pair] = unit_root(angle * (1.0 / TWO_PI))
 
     for h in range(4):
@@ -387,14 +427,26 @@
 def body(raw_pulses, range_weight, visibility, offsets, doppler_rate, phase_error, row_groups):
     first, twist, second, focus = dft_tables()
     vmem = pl.BlockSpec(memory_space=pltpu.VMEM)
-    smem = pl.BlockSpec(memory_space=pltpu.SMEM)
+    hbm = pl.BlockSpec(memory_space=pltpu.HBM)
     dma = pltpu.SemaphoreType.DMA
     focused = pl.pallas_call(
         image_kernel,
         out_shape=jax.ShapeDtypeStruct((32, 1024), F32),
-        in_specs=[smem, smem] + [vmem] * 9,
+        in_specs=[hbm] * 11,
         out_specs=vmem,
         scratch_shapes=[
+            pltpu.SMEM((32,), jnp.int32),
+            pltpu.SMEM((16, 32), F32),
+            pltpu.VMEM((2, 16, 8192), F32),
+            pltpu.VMEM((64, 128), F32),
+            pltpu.VMEM((32, 512), jnp.int32),
+            pltpu.VMEM((32, 512), jnp.int32),
+            pltpu.VMEM((4, 128), jnp.int32),
+            pltpu.VMEM((1024, 1024), BF16),
+            pltpu.VMEM((2, 64, 128), F32),
+            pltpu.VMEM((128, 256), BF16),
+            pltpu.VMEM((256, 256), BF16),
+            dma((11,)),
             pltpu.VMEM((1024, 256), BF16),
             pltpu.VMEM((1024, 256), F32),
             pltpu.VMEM((2048, 256), BF16),
@@ -412,15 +464,15 @@
             pltpu.VMEM((4, 32, 1024), BF16),
             pltpu.VMEM((32, 8, 128), F32),
             pltpu.VMEM((64, 8, 128), F32),
-            dma((1,)), dma((1,)),
+            dma((1,)), dma((2,)),
             dma((4, 4)), dma((4, 4)), dma((4, 4)), dma((4, 4)),
             dma((1,)), dma((1,)),
         ],
         compiler_params=pltpu.CompilerParams(
-            collective_id=0, has_side_effects=True, vmem_limit_bytes=48 * 2**20
+            collective_id=0, has_side_effects=True, vmem_limit_bytes=62 * 2**20
         ),
     )(
-        doppler_rate, phase_error, raw_pulses, range_weight.reshape(64, 128), offsets, visibility,
+        doppler_rate, phase_error.T, raw_pulses, range_weight.reshape(64, 128), offsets, visibility,
         row_groups.reshape(4, 128), jnp.asarray(first), jnp.asarray(twist), jnp.asarray(second), jnp.asarray(focus),
     )
     return focused[None]

time: 64.8 us -> 53.4 us (0.82)
  local copies, waits for them, and re-layouts: 10.6 us -> 1.57 us
  Pallas kernels: 53.7 us -> 51.7 us
    unnamed x22 -> x1, local copies, waits for them, and re-layouts: 10.6 us -> 1.57 us
    pallas_call x1, Pallas kernels: 53.7 us -> 51.7 us  [body(): pl.pallas_call(image_kernel, out_shape=jax.ShapeDtypeStruct((32, 1024), F...]
where the time goes in v3:
time: 53.4 us; the launch traced here: 53.3 us
  Pallas kernels  51.7 us (97%)
  local copies, waits for them, and re-layouts  1.57 us (3%)
    pallas_call x1, Pallas kernels, body(): pl.pallas_call(image_kernel, out_shape=jax.ShapeDtypeStruct((32, 1024), F...  51.7 us
    unnamed x1, local copies, waits for them, and re-layouts  1.57 us

profile of v3, /device:TPU:1, one launch (start us, length us, event | category | flops | bytes accessed | tf_op | source)
XLA Modules:
  0.0 53.3 jit_solution(6361849294257393486)
XLA Ops:
  0.0 51.7 %shard_map.109 = f32[32,1024]{1,0:T(8,128)} custom-call(s32[32]{0:T(128)} %rate_in.1, f32[16,32]{1,0:T(8,128)} %bitcast.6, f32[2,16,8192]{2,1,0:T(8,128)} %raw_in.1, f32[64,128]{1,0:T(8,128)} %bitcast.5, s32[32,512]{1,0:T(8,128)} %offset_in.1, s32[32,512]{1,0:T(8,128)} %seen_in.1, s32[4,128]{1,0:T(4,128)} %bitcast.7, ...), custom_call_target="tpu_custom_call" | custom-call | tf_op jit(solution)/shard_map/pallas_call | solution.py:432
  51.7 1.6 %copy.13 = f32[1,32,1024]{2,1,0:T(8,128)} copy(f32[1,32,1024]{2,1,0:T(8,128)} %bitcast.4) | data formatting | bytes 262144

commit v4 on v3

--- a/solution.py
+++ b/solution.py
@@ -73,8 +73,8 @@
     rate_ref, error_ref, raw_ref, taper_ref, offset_ref, seen_ref, group_ref,
     first_ref, twist_ref, second_ref, focus_ref, sem_in,
     signal, mid, terms, msg, recv, pick, gath, weight, phase, part_a, part_b,
-    send_a, send_b, recv_a, recv_b, msg2, recv2,
-    sem_s1, sem_r1, sem_sa, sem_ra, sem_sb, sem_rb, sem_s2, sem_r2,
+    send_a, send_b, recv_a, recv_b, send_f, recv_f, msg2, recv2,
+    sem_s1, sem_r1, sem_sa, sem_ra, sem_sb, sem_rb, sem_sf, sem_rf, sem_s2, sem_r2,
 ):
     py = lax.axis_index("pulse")
     zc = lax.axis_index("tile")
@@ -90,6 +90,8 @@
     own_slot = (((py & 1) * 4 + wx) * 4 + zb * 2 + core) * 2 + (py >> 1)
     up = (py, (zc + 4) & 31, wx)
     down = (py, (zc + 28) & 31, wx)
+    up2 = (py, (zc + 8) & 31, wx)
+    down2 = (py, (zc + 24) & 31, wx)
 
     loads = [
         pltpu.make_async_copy(a, b, sem_in.at[i])
@@ -105,8 +107,8 @@
     barrier = pltpu.get_barrier_semaphore()
     for d in PEERS:
         pl.semaphore_signal(barrier, inc=1, device_id=peer(d)[0], device_id_type=MESH)
-    pl.semaphore_signal(barrier, inc=1, device_id=up, device_id_type=MESH)
-    pl.semaphore_signal(barrier, inc=1, device_id=down, device_id_type=MESH)
+    for where in (up2, down2, up, down):
+        pl.semaphore_signal(barrier, inc=1, device_id=where, device_id_type=MESH)
 
     for i in (0, 2):
         loads[i].wait()
@@ -145,10 +147,10 @@
         terms[pl.ds(at + 16, 16), 128:256] = (-b_re).astype(BF16)
         return carry
 
-    lax.fori_loop(0, 64, turn, 0, unroll=4)
-
-    def spectrum(n, carry):
-        rows = terms[pl.ds(pl.multiple_of(n * 256, 256), 256), :]
+    lax.fori_loop(0, 64, turn, 0, unroll=8)
+
+    for n in range(8):
+        rows = terms[n * 256:n * 256 + 256, :]
         x = lax.dot_general(
             second_ref[...], rows, (((1,), (1,)), ((), ())), preferred_element_type=F32
         ) * (1.0 / math.sqrt(8192))
@@ -156,11 +158,8 @@
             blocks = swap_bits([x[a * 32:a * 32 + 32, g * 128:g * 128 + 128] for a in range(4)], 5)
             for i in range(4):
                 msg[n * 8 + g * 4 + i] = blocks[i].astype(BF16)
-        return carry
-
-    lax.fori_loop(0, 8, spectrum, 0)
-
-    pl.semaphore_wait(barrier, 65)
+
+    pl.semaphore_wait(barrier, 67)
 
     parity = py & 1
     for d in PEERS_BY_PARITY:
@@ -257,11 +256,8 @@
         gather(parity, part)
         return carry
 
-    def gather_late(part, carry):
-        gather(1 - parity, (far + part) & 3)
-        return carry
-
     far = ((zp + 4) & 7) >> 1
+    side = jnp.where((zp & 1) == 1, 1, 3)
     half_first(parity).wait_recv()
     lax.fori_loop(0, 4, gather_early, 0)
     half_first(1 - parity).wait_recv()
@@ -312,27 +308,40 @@
     def copy_b(step, h):
         return ring_copy(send_b, recv_b, sem_sb, sem_rb, step, h, down)
 
+    def copy_far(k, h):
+        rows, lanes = PIECES[h]
+        return pltpu.make_async_remote_copy(
+            src_ref=send_f.at[rows, lanes], dst_ref=recv_f.at[rows, lanes],
+            send_sem=sem_sf.at[h], recv_sem=sem_rf.at[h],
+            device_id=(up2, down2)[k], device_id_type=MESH,
+        )
+
     partial_image((zp + 4) & 7, part_a)
     for h in range(4):
         rows, lanes = PIECES[h]
-        send, copy = (send_a, copy_a) if h < 2 else (send_b, copy_b)
-        send[0, rows, lanes] = part_a[rows, lanes].astype(BF16)
-        copy(0, h).start()
-    lax.fori_loop(1, 4, gather_late, 0)
-    for s in range(1, 4):
-        partial_image((zp + 4 - s) & 7, part_a)
-        partial_image((zp + 4 + s) & 7, part_b)
+        send_f[rows, lanes] = part_a[rows, lanes].astype(BF16)
+        copy_far(h // 2, h).start()
+    gather(1 - parity, (far + side) & 3)
+    for s in range(3):
+        partial_image((zp + 3 - s) & 7, part_a)
+        partial_image((zp + 5 + s) & 7, part_b)
         for h in range(4):
             rows, lanes = PIECES[h]
-            for part, send, got, copy, late in (
-                (part_a, send_a, recv_a, copy_a, h < 2), (part_b, send_b, recv_b, copy_b, h >= 2)
+            for k, (part, send, got, copy) in enumerate(
+                ((part_a, send_a, recv_a, copy_a), (part_b, send_b, recv_b, copy_b))
             ):
                 total = part[rows, lanes]
-                if s > 1 or late:
+                if s > 0:
+                    if s == 1 and h // 2 == k:
+                        copy_far(k, h).wait_recv()
+                        total = total + recv_f[rows, lanes].astype(F32)
                     copy(s - 1, h).wait_recv()
                     total = total + got[s - 1, rows, lanes].astype(F32)
                 send[s, rows, lanes] = total.astype(BF16)
                 copy(s, h).start()
+        if s == 0:
+            gather(1 - parity, (far + 2) & 3)
+            gather(1 - parity, (far - side) & 3)
     partial_image(zp, part_a)
 
     top = lax.broadcasted_iota(jnp.int32, (8, 128), 0) < 4
@@ -348,10 +357,10 @@
 
     for h in range(4):
         rows, lanes = PIECES[h]
-        copy_a(3, h).wait_recv()
-        copy_b(3, h).wait_recv()
+        copy_a(2, h).wait_recv()
+        copy_b(2, h).wait_recv()
         part_a[rows, lanes] = (
-            part_a[rows, lanes] + recv_a[3, rows, lanes].astype(F32) + recv_b[3, rows, lanes].astype(F32)
+            part_a[rows, lanes] + recv_a[2, rows, lanes].astype(F32) + recv_b[2, rows, lanes].astype(F32)
         )
 
     rights = []
@@ -364,31 +373,33 @@
                 c, s = turns[q, pair]
                 rights.append(jnp.concatenate([i_re * c - i_im * s, i_re * s + i_im * c], axis=1))
     right = (jnp.concatenate(rights, axis=0) * (1.0 / 1024)).astype(BF16)
-    spun = lax.dot_general(focus_ref[...], right, (((1,), (1,)), ((), ())), preferred_element_type=F32)
-    for w in range(4):
+    mid[0:256, 0:128] = lax.dot_general(
+        focus_ref[...], right, (((1,), (1,)), ((), ())), preferred_element_type=F32
+    )
+    for dw in (2, 1, 3, 0):
+        w = (wx + dw) & 3
         blocks = []
         for i in range(8):
-            at = (i // 4) * 128 + w * 32 + (i % 4) * 8
-            blocks.append(spun[at:at + 8, :])
+            at = pl.multiple_of((i // 4) * 128 + w * 32 + (i % 4) * 8, 8)
+            blocks.append(mid[pl.ds(at, 8), 0:128])
         blocks = swap_bits(blocks, 3)
         for i in range(8):
             msg2[(i // 2) * 8 + w * 2 + i % 2] = blocks[i]
-
-    for d in PEERS:
-        where, _, index = peer(d)
-        pltpu.make_async_remote_copy(
-            src_ref=msg2.at[index], dst_ref=recv2.at[me], send_sem=sem_s2.at[0], recv_sem=sem_r2.at[0],
-            device_id=where, device_id_type=MESH,
-        ).start()
+        for d in PEERS:
+            if (d >> 1) & 3 == dw:
+                where, _, index = peer(d)
+                pltpu.make_async_remote_copy(
+                    src_ref=msg2.at[index], dst_ref=recv2.at[me], send_sem=sem_s2.at[0], recv_sem=sem_r2.at[0],
+                    device_id=where, device_id_type=MESH,
+                ).start()
     recv2[me] = msg2[py * 8 + wx * 2 + zb]
 
     all_first.wait_send()
-    for s in range(4):
-        for h in range(4):
-            if s > 0 or h < 2:
-                copy_a(s, h).wait_send()
-            if s > 0 or h >= 2:
-                copy_b(s, h).wait_send()
+    for h in range(4):
+        copy_far(h // 2, h).wait_send()
+        for s in range(3):
+            copy_a(s, h).wait_send()
+            copy_b(s, h).wait_send()
     all_last = pltpu.make_async_remote_copy(
         src_ref=recv2.at[pl.ds(0, 63)], dst_ref=recv2.at[pl.ds(0, 63)], send_sem=sem_s2.at[0], recv_sem=sem_r2.at[0],
         device_id=peer(1)[0], device_id_type=MESH,
@@ -458,14 +469,17 @@
             pltpu.VMEM((32, 4, 16, 128), F32),
             pltpu.VMEM((32, 1024), F32),
             pltpu.VMEM((32, 1024), F32),
-            pltpu.VMEM((4, 32, 1024), BF16),
-            pltpu.VMEM((4, 32, 1024), BF16),
-            pltpu.VMEM((4, 32, 1024), BF16),
-            pltpu.VMEM((4, 32, 1024), BF16),
+            pltpu.VMEM((3, 32, 1024), BF16),
+            pltpu.VMEM((3, 32, 1024), BF16),
+            pltpu.VMEM((3, 32, 1024), BF16),
+            pltpu.VMEM((3, 32, 1024), BF16),
+            pltpu.VMEM((32, 1024), BF16),
+            pltpu.VMEM((32, 1024), BF16),
             pltpu.VMEM((32, 8, 128), F32),
             pltpu.VMEM((64, 8, 128), F32),
             dma((1,)), dma((2,)),
-            dma((4, 4)), dma((4, 4)), dma((4, 4)), dma((4, 4)),
+            dma((3, 4)), dma((3, 4)), dma((3, 4)), dma((3, 4)),
+            dma((4,)), dma((4,)),
             dma((1,)), dma((1,)),
         ],
         compiler_params=pltpu.CompilerParams(

time: 53.4 us -> 52 us (0.974)
  Pallas kernels: 51.7 us -> 50.3 us
    pallas_call x1, Pallas kernels: 51.7 us -> 50.3 us  [body(): pl.pallas_call(image_kernel, out_shape=jax.ShapeDtypeStruct((32, 1024), F...]
where the time goes in v4:
time: 52 us; the launch traced here: 51.8 us
  Pallas kernels  50.3 us (97%)
  local copies, waits for them, and re-layouts  1.57 us (3%)
    pallas_call x1, Pallas kernels, body(): pl.pallas_call(image_kernel, out_shape=jax.ShapeDtypeStruct((32, 1024), F...  50.3 us
    unnamed x1, local copies, waits for them, and re-layouts  1.57 us

profile of v4, /device:TPU:1, one launch (start us, length us, event | category | flops | bytes accessed | tf_op | source)
XLA Modules:
  0.0 51.8 jit_solution(10498157941754051612)
XLA Ops:
  0.0 50.3 %shard_map.109 = f32[32,1024]{1,0:T(8,128)} custom-call(s32[32]{0:T(128)} %rate_in.1, f32[16,32]{1,0:T(8,128)} %bitcast.6, f32[2,16,8192]{2,1,0:T(8,128)} %raw_in.1, f32[64,128]{1,0:T(8,128)} %bitcast.5, s32[32,512]{1,0:T(8,128)} %offset_in.1, s32[32,512]{1,0:T(8,128)} %seen_in.1, s32[4,128]{1,0:T(4,128)} %bitcast.7, ...), custom_call_target="tpu_custom_call" | custom-call | tf_op jit(solution)/shard_map/pallas_call | solution.py:443
  50.3 1.6 %copy.13 = f32[1,32,1024]{2,1,0:T(8,128)} copy(f32[1,32,1024]{2,1,0:T(8,128)} %bitcast.4) | data formatting | bytes 262144

commit v5 on v4

--- a/solution.py
+++ b/solution.py
@@ -385,13 +385,12 @@
         blocks = swap_bits(blocks, 3)
         for i in range(8):
             msg2[(i // 2) * 8 + w * 2 + i % 2] = blocks[i]
-        for d in PEERS:
-            if (d >> 1) & 3 == dw:
-                where, _, index = peer(d)
-                pltpu.make_async_remote_copy(
-                    src_ref=msg2.at[index], dst_ref=recv2.at[me], send_sem=sem_s2.at[0], recv_sem=sem_r2.at[0],
-                    device_id=where, device_id_type=MESH,
-                ).start()
+    for d in PEERS:
+        where, _, index = peer(d)
+        pltpu.make_async_remote_copy(
+            src_ref=msg2.at[index], dst_ref=recv2.at[me], send_sem=sem_s2.at[0], recv_sem=sem_r2.at[0],
+            device_id=where, device_id_type=MESH,
+        ).start()
     recv2[me] = msg2[py * 8 + wx * 2 + zb]
 
     all_first.wait_send()

time: 52 us -> 51.9 us (level)
  no operation moved by 1% of the time
where the time goes in v5:
time: 51.9 us; the launch traced here: 51.7 us
  Pallas kernels  50.2 us (97%)
  local copies, waits for them, and re-layouts  1.57 us (3%)
    pallas_call x1, Pallas kernels, body(): pl.pallas_call(image_kernel, out_shape=jax.ShapeDtypeStruct((32, 1024), F...  50.2 us
    unnamed x1, local copies, waits for them, and re-layouts  1.57 us

profile of v5, /device:TPU:1, one launch (start us, length us, event | category | flops | bytes accessed | tf_op | source)
XLA Modules:
  0.0 51.7 jit_solution(1810980575580543046)
XLA Ops:
  0.0 50.2 %shard_map.109 = f32[32,1024]{1,0:T(8,128)} custom-call(s32[32]{0:T(128)} %rate_in.1, f32[16,32]{1,0:T(8,128)} %bitcast.6, f32[2,16,8192]{2,1,0:T(8,128)} %raw_in.1, f32[64,128]{1,0:T(8,128)} %bitcast.5, s32[32,512]{1,0:T(8,128)} %offset_in.1, s32[32,512]{1,0:T(8,128)} %seen_in.1, s32[4,128]{1,0:T(4,128)} %bitcast.7, ...), custom_call_target="tpu_custom_call" | custom-call | tf_op jit(solution)/shard_map/pallas_call | solution.py:442
  50.2 1.6 %copy.13 = f32[1,32,1024]{2,1,0:T(8,128)} copy(f32[1,32,1024]{2,1,0:T(8,128)} %bitcast.4) | data formatting | bytes 262144
